TPU v7x, 256 devices: a whole 4x4x8 slice. The times are simulated.
256 devices in a mesh: gx: 32 (over x, z), gy: 8 (over y, core).
Axes of the slice: x: 4, y: 4, z: 8, core: 2. Of those that a mesh axis runs over, the one named last changes fastest.
Arguments:
- positions: float32 [3, 2097152], P(None, ('gx', 'gy')), as said below
- velocities: float32 [3, 2097152], P(None, ('gx', 'gy')), may hold values from -3 to 3
- angular_velocity: float32 [3, 2097152], P(None, ('gx', 'gy')), may hold values from -6 to 6
- radius: float32 [2097152], P(('gx', 'gy')), may hold values from 0.3 to 0.5
- cell_index: int32 [2097152], P(('gx', 'gy')), may hold values from 0 to 2047, as said below
- pair_index: int32 [16384, 2, 128], P(('gx', 'gy')), may hold values from 0 to 10239, as said below
- live_blocks: int32 [256], P(('gx', 'gy')), may hold values from 8 to 32, as said below
- fluid_velocity: float32 [3, 64, 64, 128], P(None, 'gx', 'gy')
Outputs:
- particle_force: float32 [3, 2097152], P(None, ('gx', 'gy'))
- particle_torque: float32 [3, 2097152], P(None, ('gx', 'gy'))
- pressure: float32 [64, 64, 128], P('gx', 'gy')
Inputs may be any that keep to these rules, and one draw needn't show every extreme that they name: `cell_index`: the cell lies in the device's block; the first 2048 particles of every device lie in the block's last layer along the first dimension. `positions`: each particle lies inside the unit cube of its cell (cells are unit cubes, the grid starts at 0). `pair_index`: A first entry names a particle of the device. A second entry names another particle of the device in the same cell, or, at 8192 + k, particle k of the device one lower along gx with the same gy index, in the cell beside the first particle's along the first dimension; devices at gx index 0 name no such particle. Entries of blocks that are not live are valid too. `live_blocks`: some device has exactly 32 blocks live.
All inputs are finite; a program needn't handle non-finite values.
Results may differ from a plain program's by a relative error of at most 0.0003.
Values sent between devices are 32-bit elements; how exact they have to be, the bound alone decides.
No kernel may reach another device: no remote copies, remote signals or barrier semaphores. Data moves between devices by JAX's collectives and lax.ppermute only.
A program may use at most 128 MiB of HBM per device.

v0:
```python
import jax
import jax.numpy as jnp
from jax import lax
from jax.sharding import PartitionSpec as P

ITERS = 3


STIFFNESS = 4.0
DAMPING = 1.0
FRICTION = 0.5
SLIP_SCALE = 0.1
DRAG_RATE = 3.0
SPHERE = 4.18879020478639


def padded_2(block, sides, width):
    for axis, dim in sides:
        count = lax.axis_size(axis)
        forward = [(i, i + 1) for i in range(count - 1)]
        backward = [(target, source) for source, target in forward]
        low = lax.ppermute(
            lax.slice_in_dim(block, block.shape[dim] - width, None, axis=dim), axis, forward
        )
        high = lax.ppermute(lax.slice_in_dim(block, 0, width, axis=dim), axis, backward)
        block = jnp.concatenate([low, block, high], axis=dim)
    return block


def from_behind(value, axis, steps):
    count = lax.axis_size(axis)
    initial, last = (max(0, -steps), min(count, count - steps))
    return lax.ppermute(value, axis, [(source, source + steps) for source in range(initial, last)])


def cross_product(left, right):
    return jnp.stack(
        [
            left[1] * right[2] - left[2] * right[1],
            left[2] * right[0] - left[0] * right[2],
            left[0] * right[1] - left[1] * right[0],
        ]
    )


def contact_terms(
    pos_first, pos_second, vel_first, vel_second, spin_first, spin_second, rad_first, rad_second
):
    offset = pos_second - pos_first
    distance = jnp.sqrt(jnp.sum(offset * offset, axis=0))
    contact_reach = rad_first + rad_second
    normal = offset / jnp.maximum(distance, 0.25 * contact_reach)
    correlation = jnp.maximum(contact_reach - distance, 0.0)
    root_correlation = jnp.sqrt(correlation)
    lever_arm = rad_first * spin_first + rad_second * spin_second
    slip_velocity = vel_second - vel_first - cross_product(lever_arm, normal)
    normal_speed = jnp.sum(slip_velocity * normal, axis=0)
    normal_push = (
        STIFFNESS * correlation * root_correlation - DAMPING * root_correlation * normal_speed
    )
    tangent = slip_velocity - normal_speed * normal
    tangent_size = jnp.sqrt(jnp.sum(tangent * tangent, axis=0) + SLIP_SCALE * SLIP_SCALE)
    friction = FRICTION * jnp.abs(normal_push) * tangent / tangent_size
    pair_force = friction - normal_push * normal
    pair_twist = cross_product(normal, friction)
    return (pair_force, rad_first * pair_twist, rad_second * pair_twist)


def faces_of(padded):
    return [
        padded[2:, 1:-1, 1:-1],
        padded[:-2, 1:-1, 1:-1],
        padded[1:-1, 2:, 1:-1],
        padded[1:-1, :-2, 1:-1],
        padded[1:-1, 1:-1, 2:],
        padded[1:-1, 1:-1, :-2],
    ]


def operate(field, porosity, padded_porosity):
    padded_field = padded_2(field, (("gx", 0), ("gy", 1)), 1)
    padded_field = jnp.pad(padded_field, ((0, 0), (0, 0), (1, 1)))
    result = jnp.zeros_like(field)
    for near_field, near_porosity in zip(faces_of(padded_field), faces_of(padded_porosity)):
        result = result + 0.5 * (porosity + near_porosity) * (field - near_field)
    return result


def squared_total(residual):
    return lax.psum(jnp.sum(residual * residual), ("gx", "gy"))


def per_device(
    positions,
    velocities,
    angular_velocity,
    radius,
    cell_index,
    pair_index,
    live_blocks,
    fluid_velocity,
):
    own_count = positions.shape[1]
    cells_x = fluid_velocity.shape[1]
    cells_y = fluid_velocity.shape[2]
    cells_z = fluid_velocity.shape[3]
    border = 2 * cells_y * cells_z
    outgoing = jnp.concatenate(
        [
            positions[:, :border],
            velocities[:, :border],
            angular_velocity[:, :border],
            radius[None, :border],
        ],
        0,
    )
    ghosts = from_behind(outgoing, "gx", 1)
    every_position = jnp.concatenate([positions, ghosts[0:3]], 1)
    every_velocity = jnp.concatenate([velocities, ghosts[3:6]], 1)
    every_spin = jnp.concatenate([angular_velocity, ghosts[6:9]], 1)
    every_radius = jnp.concatenate([radius, ghosts[9]], 0)
    live_count = live_blocks[0]
    empty_accum = jnp.zeros((6, own_count + border), jnp.float32)
    accum = empty_accum
    span_blocks = pair_index.shape[0]
    first = pair_index[:, 0, :].reshape(-1)
    second = pair_index[:, 1, :].reshape(-1)
    block_ids = jnp.arange(span_blocks, dtype=jnp.int32)
    keep = jnp.broadcast_to((block_ids < live_count)[:, None], (span_blocks, pair_index.shape[2]))
    keep = keep.reshape(-1).astype(jnp.float32)
    pair_force, twist_first, twist_second = contact_terms(
        every_position[:, first],
        every_position[:, second],
        every_velocity[:, first],
        every_velocity[:, second],
        every_spin[:, first],
        every_spin[:, second],
        every_radius[first],
        every_radius[second],
    )
    accum = accum.at[:, first].add(jnp.concatenate([pair_force * keep, twist_first * keep], 0))
    accum = accum.at[:, second].add(jnp.concatenate([-pair_force * keep, twist_second * keep], 0))
    returned = from_behind(accum[:, own_count:], "gx", -1)
    own_terms = jnp.concatenate([accum[:, :border] + returned, accum[:, border:own_count]], 1)
    fluid_flat = fluid_velocity.reshape(3, -1)
    drag = DRAG_RATE * radius * (fluid_flat[:, cell_index] - velocities)
    particle_force = own_terms[:3] + drag
    particle_torque = own_terms[3:]
    deposit = (
        jnp.zeros((4, cells_x * cells_y * cells_z), jnp.float32)
        .at[:, cell_index]
        .add(jnp.concatenate([-drag, (SPHERE * radius * radius * radius)[None]], 0))
    )
    porosity = (1.0 / (1.0 + deposit[3])).reshape(cells_x, cells_y, cells_z)
    fields = jnp.stack(
        [
            porosity,
            deposit[0].reshape(cells_x, cells_y, cells_z),
            deposit[1].reshape(cells_x, cells_y, cells_z),
        ]
    )
    rimmed = padded_2(fields, (("gx", 1), ("gy", 2)), 1)
    rimmed = jnp.pad(rimmed, ((0, 0), (0, 0), (0, 0), (1, 1)))
    depth_padded = jnp.pad(deposit[2].reshape(cells_x, cells_y, cells_z), ((0, 0), (0, 0), (1, 1)))
    source = 0.5 * (rimmed[1, 2:, 1:-1, 1:-1] - rimmed[1, :-2, 1:-1, 1:-1])
    source = source + 0.5 * (rimmed[2, 1:-1, 2:, 1:-1] - rimmed[2, 1:-1, :-2, 1:-1])
    source = source + 0.5 * (depth_padded[:, :, 2:] - depth_padded[:, :, :-2])
    padded_porosity = rimmed[0]
    pressure = jnp.zeros_like(source)
    residual = source
    direction = source
    norm_now = squared_total(residual)
    for iteration in range(ITERS):
        image = operate(direction, porosity, padded_porosity)
        curvature = lax.psum(jnp.sum(direction * image), ("gx", "gy"))
        alpha = norm_now / curvature
        pressure = pressure + alpha * direction
        residual = residual - alpha * image
        norm_next = squared_total(residual)
        direction = residual + norm_next / norm_now * direction
        norm_now = norm_next
    return (particle_force, particle_torque, pressure)


def solution(mesh):
    return jax.shard_map(
        per_device,
        mesh=mesh,
        in_specs=(
            P(None, ("gx", "gy")),
            P(None, ("gx", "gy")),
            P(None, ("gx", "gy")),
            P(("gx", "gy")),
            P(("gx", "gy")),
            P(("gx", "gy"), None, None),
            P(("gx", "gy")),
            P(None, "gx", "gy", None),
        ),
        out_specs=(P(None, ("gx", "gy")), P(None, ("gx", "gy")), P("gx", "gy", None)),
        check_vma=False,
    )
```

profile of v0, /device:TPU:1, one launch (start us, length us, event | category | flops | bytes accessed | tf_op | source)
XLA Modules:
  0.0 959.6 jit_solution(6183412301435894593)
XLA Ops:
  3.7 4.4 collective-permute-start
  13.7 3.1 copy.78
  16.8 30.2 %gather_fusion.2 = f32[8192,3]{1,0:T(8,128)} fusion(f32[3,10240]{0,1:T(8,128)} %copy.78, s32[8192]{0:T(1024)S(1)} %broadcast_clamp_fusion.1), kind=kCustom, calls=%fused_computation.2 | custom fusion | bytes 229376 | tf_op jit(solution)/shard_map/gather | solution.py:133
  47.0 30.2 %gather_fusion.3 = f32[8192,3]{1,0:T(8,128)} fusion(f32[3,10240]{0,1:T(8,128)} %copy.78, s32[8192]{0:T(1024)S(1)} %broadcast_clamp_fusion.2), kind=kCustom, calls=%fused_computation.3 | custom fusion | bytes 229376 | tf_op jit(solution)/shard_map/gather | solution.py:132
  77.2 45.5 %gather_fusion = f32[8192]{0:T(1024)S(1)} fusion(f32[10240]{0:T(1024)S(1)} %pad_maximum_fusion.6, s32[8192]{0:T(1024)S(1)} %broadcast_clamp_fusion.2), kind=kCustom, calls=%fused_computation | custom fusion | bytes 98304 | tf_op jit(solution)/shard_map/gather | solution.py:138
  122.7 45.5 %gather_fusion.1 = f32[8192]{0:T(1024)S(1)} fusion(f32[10240]{0:T(1024)S(1)} %pad_maximum_fusion.6, s32[8192]{0:T(1024)S(1)} %broadcast_clamp_fusion.1), kind=kCustom, calls=%fused_computation.1 | custom fusion | bytes 98304 | tf_op jit(solution)/shard_map/gather | solution.py:139
  168.3 3.1 copy.86
  171.5 30.2 %gather_fusion.6 = f32[8192,3]{1,0:T(8,128)} fusion(f32[3,10240]{0,1:T(8,128)} %copy.86, s32[8192]{0:T(1024)S(1)} %broadcast_clamp_fusion.2), kind=kCustom, calls=%fused_computation.6 | custom fusion | bytes 229376 | tf_op jit(solution)/shard_map/gather | solution.py:136
  201.7 30.2 %gather_fusion.7 = f32[8192,3]{1,0:T(8,128)} fusion(f32[3,10240]{0,1:T(8,128)} %copy.86, s32[8192]{0:T(1024)S(1)} %broadcast_clamp_fusion.1), kind=kCustom, calls=%fused_computation.7 | custom fusion | bytes 229376 | tf_op jit(solution)/shard_map/gather | solution.py:137
  231.9 3.1 copy.82
  235.0 30.2 %gather_fusion.4 = f32[8192,3]{1,0:T(8,128)} fusion(f32[3,10240]{0,1:T(8,128)} %copy.82, s32[8192]{0:T(1024)S(1)} %broadcast_clamp_fusion.1), kind=kCustom, calls=%fused_computation.4 | custom fusion | bytes 229376 | tf_op jit(solution)/shard_map/gather | solution.py:135
  265.2 30.2 %gather_fusion.5 = f32[8192,3]{1,0:T(8,128)} fusion(f32[3,10240]{0,1:T(8,128)} %copy.82, s32[8192]{0:T(1024)S(1)} %broadcast_clamp_fusion.2), kind=kCustom, calls=%fused_computation.5 | custom fusion | bytes 229376 | tf_op jit(solution)/shard_map/gather | solution.py:134
  309.6 2.9 copy.85
  319.4 46.9 %scatter_custom_fusion = f32[6,10240]{0,1:T(8,128)} fusion(s32[8192]{0:T(1024)S(1)} %bitcast.116, f32[8192,6]{1,0:T(8,128)} %copy.90, f32[]{:T(128)} %constant.11.clone.1), kind=kCustom, calls=%fused_computation.12 | custom fusion | flops 49152 | bytes 246272 | tf_op jit(solution)/shard_map/scatter-add | solution.py:141
  366.4 44.7 %scatter_fusion = f32[6,10240]{0,1:T(8,128)} fusion(f32[6,10240]{0,1:T(8,128)} %scatter_custom_fusion, s32[8192]{0:T(1024)S(1)} %bitcast.105, f32[8192,6]{1,0:T(8,128)} %copy.91), kind=kCustom, calls=%fused_computation.10 | custom fusion | flops 49152 | bytes 622592 | tf_op jit(solution)/shard_map/scatter-add | solution.py:142
  416.9 27.7 %gather_fusion.8 = f32[8192,3]{1,0:T(8,128)} fusion(f32[3,2048]{0,1:T(8,128)S(1)} %bitcast.99, s32[8192]{0:T(1024)S(1)} %get-tuple-element.58), kind=kCustom, calls=%fused_computation.8 | custom fusion | bytes 229376 | tf_op jit(solution)/shard_map/gather | solution.py:146
  444.6 3.5 copy.96
  459.0 44.5 %scatter_custom_fusion.2 = f32[4,2048]{0,1:T(8,128)S(1)} fusion(s32[8192]{0:T(1024)} %get-tuple-element.57, f32[8192,4]{1,0:T(8,128)} %copy.97, f32[]{:T(128)} %constant.11.clone.1), kind=kCustom, calls=%fused_computation.20 | custom fusion | flops 32768 | bytes 33280 | tf_op jit(solution)/shard_map/scatter-add | solution.py:152
  506.9 4.8 collective-permute-start.3
  512.5 3.8 collective-permute-start.4
  516.3 3.1 collective-permute-start.5
  521.6 4.5 collective-permute-start.7
  529.0 4.8 collective-permute-start.9
  535.6 85.8 %all-reduce.5 = (f32[]{:T(128)}, f32[]{:T(128)}) all-reduce(f32[]{:T(128)} %get-tuple-element.17, f32[]{:T(128)} %get-tuple-element.16), channel_id=1, replica_groups=mesh['gx'=32,'gy'=8] {'gx','gy'}, use_global_device_ids=true, to_apply=%region_7.8 | all-reduce | flops 2 | bytes 16 | tf_op jit(solution)/shard_map/psum | solution.py:90
  623.2 73.5 %psum.44 = f32[]{:T(128)} all-reduce(f32[]{:T(128)} %get-tuple-element.22), channel_id=1, replica_groups=mesh['gx'=32,'gy'=8] {'gx','gy'}, use_global_device_ids=true, to_apply=%region_11.12 | all-reduce | flops 1 | bytes 8 | tf_op jit(solution)/shard_map/psum | solution.py:90
  699.3 4.0 collective-permute-start.11
  704.0 3.7 collective-permute-start.12
  712.1 77.5 %psum.45 = f32[]{:T(128)} all-reduce(f32[]{:T(128)} %get-tuple-element.20), channel_id=1, replica_groups=mesh['gx'=32,'gy'=8] {'gx','gy'}, use_global_device_ids=true, to_apply=%region_13.14 | all-reduce | flops 1 | bytes 8 | tf_op jit(solution)/shard_map/psum | solution.py:175
  791.5 73.5 %psum.46 = f32[]{:T(128)} all-reduce(f32[]{:T(128)} %multiply_reduce_fusion.3), channel_id=1, replica_groups=mesh['gx'=32,'gy'=8] {'gx','gy'}, use_global_device_ids=true, to_apply=%region_15.16 | all-reduce | flops 1 | bytes 8 | tf_op jit(solution)/shard_map/psum | solution.py:90
  867.7 4.0 collective-permute-start.15
  872.4 3.7 collective-permute-start.16
  880.0 77.6 %psum.47 = f32[]{:T(128)} all-reduce(f32[]{:T(128)} %fusion.24), channel_id=1, replica_groups=mesh['gx'=32,'gy'=8] {'gx','gy'}, use_global_device_ids=true, to_apply=%region_17.18 | all-reduce | flops 1 | bytes 8 | tf_op jit(solution)/shard_map/psum | solution.py:175
  (109 shorter events, 70.9 us)
Async XLA Ops:
  3.7 8.9 collective-permute-start
  12.6 64.6 %copy-start.2 = (f32[8192]{0:T(1024)S(1)}, f32[8192]{0:T(1024)}, u32[]{:S(2)}) copy-start(f32[8192]{0:T(1024)} %param.11) | copy-start | bytes 98308
  122.7 45.6 %copy-start.1 = (f32[3,8192]{1,0:T(4,128)S(1)}, f32[3,8192]{1,0:T(4,128)}, u32[]{:S(2)}) copy-start(f32[3,8192]{1,0:T(4,128)} %param.10) | copy-start | bytes 294916
  366.4 50.2 %copy-start.3 = (f32[3,2,8,128]{3,2,1,0:T(8,128)S(1)}, f32[3,2,8,128]{3,2,1,0:T(8,128)}, u32[]{:S(2)}) copy-start(f32[3,2,8,128]{3,2,1,0:T(8,128)} %param.15) | copy-start | bytes 73732
  414.6 38.4 %collective-permute-start.1 = (f32[6,2048]{1,0:T(8,128)}, f32[6,2048]{1,0:T(8,128)}, u32[]{:S(2)}, u32[]{:S(2)}) collective-permute-start(f32[6,2048]{1,0:T(8,128)} %copy.92), channel_id=1, source_target_pairs={{8,0},{16,8},{24,16},{32,24},{40,32},{48,40},{56,48},{64,56},{72,6... | collective-permute-start | bytes 147464 | tf_op jit(solution)/shard_map/ppermute | solution.py:33
  448.1 5.7 copy-start
  505.6 6.1 collective-permute-start.2
  506.9 5.6 collective-permute-start.3
  512.5 7.0 collective-permute-start.4
  516.3 3.9 collective-permute-start.5
  520.3 5.9 collective-permute-start.6
  521.6 5.3 collective-permute-start.7
  526.9 7.8 collective-permute-start.8
  529.0 5.7 collective-permute-start.9
  698.0 5.3 collective-permute-start.10
  699.3 4.7 collective-permute-start.11
  704.0 6.5 collective-permute-start.12
  707.7 3.5 collective-permute-start.13
  866.4 5.3 collective-permute-start.14
  867.7 4.7 collective-permute-start.15
  872.4 6.1 collective-permute-start.16
  876.1 3.1 collective-permute-start.17
where the time goes:
time: 962 us; the launch traced here: 960 us
  blocking collectives  388 us (40%)
  local copies, waits for them, and re-layouts  350 us (36%)
  other arithmetic  154 us (16%)
  starting transfers between devices  54.5 us (6%)
    psum x3, blocking collectives, squared_total(): return lax.psum(jnp.sum(residual * residual), ('gx', 'gy'))  233 us
    psum x2, blocking collectives, per_device(): curvature = lax.psum(jnp.sum(direction * image), ('gx', 'gy'))  155 us
    scatter-add x1, other arithmetic, per_device(): accum.at[:, first]  46.9 us
    gather x1, local copies, waits for them, and re-layouts, per_device(): every_radius[second]  45.5 us
    gather x1, local copies, waits for them, and re-layouts, per_device(): every_radius[first]  45.5 us
    scatter-add x1, other arithmetic, per_device(): accum.at[:, second]  44.7 us
    scatter-add x1, other arithmetic, per_device(): deposit = jnp.zeros((4, cells_x * cells_y * cells_z), jnp.float32).at[:,...  44.5 us
    gather x2, local copies, waits for them, and re-layouts, per_device(): every_spin[:, first]  33.1 us
  transfers between devices with their start and end apart: 18, of which 7 were waited for; matrix products, arithmetic and copies ran while one was open for 4% of the time, Pallas kernels for 0%

commit v1 on v0

v1 whole, which is shorter than its diff:
```python
import functools

import jax
import jax.numpy as jnp
from jax import lax
from jax.experimental import pallas as pl
from jax.experimental.pallas import tpu as pltpu
from jax.sharding import PartitionSpec as P

STIFFNESS = 4.0
DAMPING = 1.0
FRICTION = 0.5
SLIP_SCALE = 0.1
DRAG_RATE = 3.0
SPHERE = 4.18879020478639

F32 = jnp.float32
BF16 = jnp.bfloat16
BOTH = ("gx", "gy")
VMEM_SPEC = pl.BlockSpec(memory_space=pltpu.VMEM)
SMEM_SPEC = pl.BlockSpec(memory_space=pltpu.SMEM)
PARAMS = pltpu.CompilerParams(vmem_limit_bytes=24 * 1024 * 1024)


def split(x):
    high = x.astype(BF16)
    return high, (x - high.astype(F32)).astype(BF16)


def one_hot(size, index):
    rows = lax.broadcasted_iota(jnp.int32, (size, index.shape[1]), 0)
    return rows == index


def as_bf16(mask):
    return jnp.where(mask, 1.0, 0.0).astype(BF16)


def lanes(block, rows):
    return jnp.concatenate([block[r : r + 1, :] for r in rows], axis=1)


def dot_nt(left, right):
    return lax.dot_general(left, right, (((1,), (1,)), ((), ())), preferred_element_type=F32)


def deposit_kernel(vel, radius, cell, fluid, fields, drag):
    fluid_high, fluid_low = split(fluid[...])
    fluid_table = jnp.concatenate([fluid_high, fluid_low], axis=1)
    total = jnp.zeros((64, 128), F32)
    for g in range(8):
        cells = lanes(cell[8 * g : 8 * g + 8, :], range(8))
        rad = lanes(radius[8 * g : 8 * g + 8, :], range(8))
        here = pl.ds(1024 * g, 1024)
        hot = as_bf16(one_hot(128, cells & 127))
        mask = one_hot(16, cells >> 7)
        seen = jnp.dot(
            fluid_table, jnp.concatenate([hot, hot], axis=0), preferred_element_type=F32
        )
        values = []
        for d in range(3):
            u = jnp.sum(jnp.where(mask, seen[16 * d : 16 * d + 16], 0.0), axis=0, keepdims=True)
            force = DRAG_RATE * rad * (u - vel[d : d + 1, here])
            drag[d : d + 1, here] = force
            values.append(-force)
        values.append(SPHERE * rad * rad * rad)
        spread = jnp.concatenate([jnp.where(mask, v, 0.0) for v in values], axis=0)
        high, low = split(spread)
        total = total + dot_nt(
            jnp.concatenate([high, low], axis=1), jnp.concatenate([hot, hot], axis=1)
        )
    lane = lax.broadcasted_iota(jnp.int32, (16, 128), 1)
    mz = total[32:48]
    up = jnp.where(lane == 127, 0.0, pltpu.roll(mz, 127, 1))
    down = jnp.where(lane == 0, 0.0, pltpu.roll(mz, 1, 1))
    out = [total[0:16], 1.0 / (1.0 + total[48:64]), total[16:32], 0.5 * (up - down)]
    for f in range(4):
        for layer in range(2):
            fields[f, layer] = out[f][8 * layer : 8 * layer + 8]


def table_kernel(place, pos, vel, spin, radius, cell, table, border):
    def dense(ref, d):
        return jnp.concatenate(
            [ref[d : d + 1, 128 * k : 128 * k + 128] for k in range(64)], axis=0
        )

    cells = cell[...]
    rad = radius[...]
    corner = [
        place[0] * 2 + (cells >> 10),
        place[1] * 8 + ((cells >> 7) & 7),
        cells & 127,
    ]
    fields = [dense(pos, d) - corner[d].astype(F32) for d in range(3)]
    fields += [dense(vel, d) for d in range(3)]
    fields += [rad * dense(spin, d) for d in range(3)]
    fields += [rad]
    for f in range(10):
        high, low = split(fields[f])
        rows = pl.ds(32 * f, 32)
        table[rows, 0:128] = high[0:32]
        table[rows, 128:256] = high[32:64]
        table[rows, 256:384] = low[0:32]
        table[rows, 384:512] = low[32:64]
        border[f] = fields[f][0:16] - 1.0 if f == 0 else fields[f][0:16]


def cross(a, b):
    return [
        a[1] * b[2] - a[2] * b[1],
        a[2] * b[0] - a[0] * b[2],
        a[0] * b[1] - a[1] * b[0],
    ]


def dot3(a, b):
    return a[0] * b[0] + a[1] * b[1] + a[2] * b[2]


def contact_terms(first, second):
    offset = [second[d] - first[d] for d in range(3)]
    distance = jnp.sqrt(dot3(offset, offset))
    reach = first[9] + second[9]
    inverse = 1.0 / jnp.maximum(distance, 0.25 * reach)
    normal = [o * inverse for o in offset]
    correlation = jnp.maximum(reach - distance, 0.0)
    root = jnp.sqrt(correlation)
    lever = [first[6 + d] + second[6 + d] for d in range(3)]
    turn = cross(lever, normal)
    slip = [second[3 + d] - first[3 + d] - turn[d] for d in range(3)]
    speed = dot3(slip, normal)
    push = STIFFNESS * correlation * root - DAMPING * root * speed
    tangent = [slip[d] - speed * normal[d] for d in range(3)]
    size = jnp.sqrt(dot3(tangent, tangent) + SLIP_SCALE * SLIP_SCALE)
    scale = FRICTION * jnp.abs(push) / size
    friction = [scale * t for t in tangent]
    force = [friction[d] - push * normal[d] for d in range(3)]
    twist = cross(normal, friction)
    return force, twist


def contact_kernel(live, pairs, table, ghost, drag, force_out, twist_out, returned, seconds, total):
    span = 512
    seconds[0:320, :] = table[...]
    pieces = [
        jnp.concatenate([ghost[f, 0:8, :], ghost[f, 8:16, :]], axis=1) for f in range(10)
    ]
    high, low = split(jnp.concatenate(pieces, axis=0))
    seconds[320:400, 0:256] = high
    seconds[320:400, 256:512] = low
    total[...] = jnp.zeros_like(total)
    count = jnp.minimum(live[0], 64)

    def pick(seen, mask, f):
        chosen = jnp.where(mask, seen[32 * f : 32 * f + 32], 0.0)
        return chosen[0:8] + chosen[8:16] + (chosen[16:24] + chosen[24:32])

    def step(it, carry):
        block = pairs[pl.ds(pl.multiple_of(it * 8, 8), 8), :]
        index_p = lanes(block, (0, 2, 4, 6))
        index_q = lanes(block, (1, 3, 5, 7))
        low_p = (index_p & 127) + ((index_p >> 12) << 7)
        row_p = (index_p >> 7) & 31
        is_ghost = index_q >= 8192
        wrapped = index_q - 8192
        low_q = (index_q & 127) + (jnp.where(is_ghost, wrapped >> 10, index_q >> 12) << 7)
        row_q = jnp.where(is_ghost, 32 + ((wrapped >> 7) & 7), (index_q >> 7) & 31)
        hot_p = as_bf16(one_hot(256, low_p))
        hot_q = as_bf16(one_hot(256, low_q))
        seen_p = jnp.dot(
            table[...], jnp.concatenate([hot_p, hot_p], axis=0), preferred_element_type=F32
        )
        seen_q = jnp.dot(
            seconds[...], jnp.concatenate([hot_q, hot_q], axis=0), preferred_element_type=F32
        )
        mask_p = one_hot(32, row_p)
        mask_q = one_hot(32, row_q)
        mask_g = one_hot(8, row_q - 32)
        first, second = [], []
        for f in range(10):
            first.append(jnp.sum(pick(seen_p, mask_p, f), axis=0, keepdims=True))
            beyond = jnp.where(mask_g, seen_q[320 + 8 * f : 328 + 8 * f], 0.0)
            second.append(jnp.sum(pick(seen_q, mask_q, f) + beyond, axis=0, keepdims=True))
        force, twist = contact_terms(first, second)
        lane = lax.broadcasted_iota(jnp.int32, (1, span), 1)
        keep = jnp.where(4 * it + (lane >> 7) < count, 1.0, 0.0)
        to_p = [keep * v for v in force] + [keep * first[9] * v for v in twist]
        to_q = [-keep * v for v in force] + [keep * second[9] * v for v in twist]
        spread_p = jnp.concatenate([jnp.where(mask_p, v, 0.0) for v in to_p], axis=0)
        spread_q = jnp.concatenate(
            [jnp.where(mask_q, v, 0.0) for v in to_q] + [jnp.where(mask_g, v, 0.0) for v in to_q],
            axis=0,
        )
        high_p, rest_p = split(spread_p)
        high_q, rest_q = split(spread_q)
        sum_p = dot_nt(
            jnp.concatenate([high_p, rest_p], axis=1), jnp.concatenate([hot_p, hot_p], axis=1)
        )
        sum_q = dot_nt(
            jnp.concatenate([high_q, rest_q], axis=1), jnp.concatenate([hot_q, hot_q], axis=1)
        )
        total[0:192, :] += sum_p + sum_q[0:192]
        total[192:240, :] += sum_q[192:240]
        return carry

    lax.fori_loop(0, (count + 3) // 4, step, 0)
    for f in range(6):
        returned[f, 0:8, :] = total[192 + 8 * f : 200 + 8 * f, 0:128]
        returned[f, 8:16, :] = total[192 + 8 * f : 200 + 8 * f, 128:256]
    for f in range(3):
        for k in range(64):
            at = slice(128 * k, 128 * k + 128)
            side = slice(128 * (k // 32), 128 * (k // 32) + 128)
            row = 32 * f + k % 32
            force_out[f : f + 1, at] = total[row : row + 1, side] + drag[f : f + 1, at]
            twist_out[f : f + 1, at] = total[96 + row : 97 + row, side]


def border_kernel(returned, force_in, twist_in, force_out, twist_out):
    for f in range(3):
        for k in range(16):
            at = slice(128 * k, 128 * k + 128)
            force_out[f : f + 1, at] = force_in[f : f + 1, at] + returned[f, k : k + 1, :]
            twist_out[f : f + 1, at] = twist_in[f : f + 1, at] + returned[3 + f, k : k + 1, :]


def next_row(x):
    return pltpu.roll(x, x.shape[0] - 1, 0)


def last_row(x):
    return pltpu.roll(x, 1, 0)


def rows_kernel(place, own, even_side, odd_side, wide):
    even = (place[1] & 1) == 0
    sub = lax.broadcasted_iota(jnp.int32, (8, 128), 0)

    def extend(f, layer):
        e, o = even_side[f, layer], odd_side[f, layer]
        after = jnp.where(even, e, o)
        before = jnp.where(even, o, e)
        return jnp.concatenate([own[f, layer], jnp.where(sub < 4, after, before)], axis=0)

    for layer in range(2):
        wide[0, layer] = extend(0, layer)
        wide[1, layer] = extend(1, layer)
        my = extend(2, layer)
        wide[2, layer] = extend(3, layer) + 0.5 * (next_row(my) - last_row(my))


SHIFT = 3.0


def krylov_kernel(place, own, side_a, side_b, far_c, far_d, sums, basis):
    gx, gy = place[0], place[1]
    even = (gx & 1) == 0

    def layers(f):
        a = [side_a[f, s] for s in range(2)]
        b = [side_b[f, s] for s in range(2)]
        c = [far_c[f, s] for s in range(2)]
        d = [far_d[f, s] for s in range(2)]
        pick = lambda u, v: [jnp.where(even, x, y) for x, y in zip(u, v)]
        return pick(c, d) + pick(b, a) + [own[f, 0], own[f, 1]] + pick(a, b) + pick(d, c)

    mx, por, part = layers(0), layers(1), layers(2)
    row = lax.broadcasted_iota(jnp.int32, (16, 128), 0)
    lane = lax.broadcasted_iota(jnp.int32, (16, 128), 1)
    inside_y = (row < 8) | ((row < 12) & (gy < 7)) | ((row >= 12) & (gy > 0))

    def inside(l):
        x = gx * 2 + (l - 4)
        return inside_y & (x >= 0) & (x < 64)

    masks = [inside(l) for l in range(10)]
    zplus = lambda x: jnp.where(lane == 127, 0.0, pltpu.roll(x, 127, 1))
    zminus = lambda x: jnp.where(lane == 0, 0.0, pltpu.roll(x, 1, 1))
    half = [0.5 * p for p in por]
    wx = [half[l] + half[l + 1] for l in range(9)]
    wy = [h + next_row(h) for h in half]
    wy_low = [last_row(w) for w in wy]
    wz = [h + zplus(h) for h in half]
    wz_low = [h + zminus(h) for h in half]

    def apply(p, l):
        c = p[l]
        return (
            wx[l] * (c - p[l + 1])
            + wx[l - 1] * (c - p[l - 1])
            + wy[l] * (c - next_row(c))
            + wy_low[l] * (c - last_row(c))
            + wz[l] * (c - zplus(c))
            + wz_low[l] * (c - zminus(c))
        )

    v0 = {
        l: jnp.where(masks[l], part[l] + 0.5 * (mx[l + 1] - mx[l - 1]), 0.0) for l in range(1, 9)
    }
    a0 = {l: apply(v0, l) for l in range(2, 8)}
    v1 = {l: jnp.where(masks[l], a0[l] * (1.0 / SHIFT) - v0[l], 0.0) for l in a0}
    a1 = {l: apply(v1, l) for l in range(3, 7)}
    v2 = {l: jnp.where(masks[l], a1[l] * (1.0 / SHIFT) - v1[l], 0.0) for l in a1}
    a2 = {l: apply(v2, l) for l in range(4, 6)}

    def inner(p, q):
        return jnp.sum(p[4][0:8] * q[4][0:8] + p[5][0:8] * q[5][0:8], keepdims=True)

    products = [
        inner(v0, a0),
        inner(v1, a0),
        inner(v2, a0),
        inner(v1, a1),
        inner(v2, a1),
        inner(v2, a2),
        inner(v0, v0),
        inner(v1, v0),
        inner(v2, v0),
    ]
    at = lax.broadcasted_iota(jnp.int32, (8, 128), 1)
    line = jnp.zeros((8, 128), F32)
    for k, value in enumerate(products):
        line = jnp.where(at == k, value, line)
    for r in range(32):
        sums[8 * r : 8 * r + 8, :] = line
    for s in range(2):
        basis[0, s] = v0[4 + s][0:8]
        basis[1, s] = v1[4 + s][0:8]
        basis[2, s] = v2[4 + s][0:8]


def pressure_kernel(sums, basis, pressure):
    line = jnp.sum(sums[...], axis=0, keepdims=True)
    at = lax.broadcasted_iota(jnp.int32, (1, 128), 1)
    h00, h01, h02, h11, h12, h22, g0, g1, g2 = [
        jnp.sum(jnp.where(at == k, line, 0.0), axis=1, keepdims=True) for k in range(9)
    ]
    l10 = h01 / h00
    l20 = h02 / h00
    d1 = h11 - l10 * h01
    e = h12 - l10 * h02
    l21 = e / d1
    d2 = h22 - l20 * h02 - l21 * e
    y1 = g1 - l10 * g0
    y2 = g2 - l20 * g0 - l21 * y1
    c2 = y2 / d2
    c1 = y1 / d1 - l21 * c2
    c0 = g0 / h00 - l10 * c1 - l20 * c2
    for s in range(2):
        pressure[s] = c0 * basis[0, s] + c1 * basis[1, s] + c2 * basis[2, s]


def shape(*dims, dtype=F32):
    return jax.ShapeDtypeStruct(dims, dtype)


def call(kernel, out, specs, outs=None, scratch=(), cost=None, **more):
    return pl.pallas_call(
        kernel,
        out_shape=out,
        in_specs=specs,
        out_specs=outs if outs is not None else jax.tree.map(lambda _: VMEM_SPEC, out),
        scratch_shapes=scratch,
        compiler_params=PARAMS,
        cost_estimate=cost,
        **more,
    )


def swaps(count):
    even = [(i, i ^ 1) for i in range(count)]
    odd = [(i, ((i + 1) ^ 1) - 1) for i in range(1, count - 1)]
    return even, odd


def per_device(pos, vel, spin, radius, cell, pairs, live, fluid):
    place = jnp.stack([lax.axis_index("gx"), lax.axis_index("gy")]).astype(jnp.int32)
    radius = radius.reshape(64, 128)
    cell = cell.reshape(64, 128)
    pairs = pairs.reshape(128, 128)
    fluid = fluid.reshape(48, 128)
    even_x, odd_x = swaps(32)
    even_y, odd_y = swaps(8)

    fields, drag = call(
        deposit_kernel, (shape(4, 2, 8, 128), shape(3, 8192)), [VMEM_SPEC] * 4
    )(vel, radius, cell, fluid)
    table, border = call(
        table_kernel,
        (shape(320, 512, dtype=BF16), shape(10, 16, 128)),
        [SMEM_SPEC] + [VMEM_SPEC] * 5,
    )(place, pos, vel, spin, radius, cell)

    even_side = lax.ppermute(fields, "gy", even_y)
    odd_side = lax.ppermute(fields, "gy", odd_y)
    ghost = lax.ppermute(border, "gx", [(i, i + 1) for i in range(31)])
    wide = call(rows_kernel, shape(3, 2, 16, 128), [SMEM_SPEC] + [VMEM_SPEC] * 3)(
        place, fields, even_side, odd_side
    )
    side_a = lax.ppermute(wide, "gx", even_x)
    side_b = lax.ppermute(wide, "gx", odd_x)
    far_c = lax.ppermute(side_a, "gx", odd_x)
    far_d = lax.ppermute(side_b, "gx", even_x)
    sums, basis = call(
        krylov_kernel, (shape(256, 128), shape(3, 2, 8, 128)), [SMEM_SPEC] + [VMEM_SPEC] * 5
    )(place, wide, side_a, side_b, far_c, far_d)
    every = lax.all_to_all(sums, BOTH, 0, 0, tiled=True)

    force, twist, back = call(
        contact_kernel,
        (shape(3, 8192), shape(3, 8192), shape(6, 16, 128)),
        [SMEM_SPEC] + [VMEM_SPEC] * 4,
        scratch=[pltpu.VMEM((400, 512), BF16), pltpu.VMEM((240, 256), F32)],
        cost=pl.CostEstimate(flops=5 * 10**9, bytes_accessed=10**6, transcendentals=0),
    )(live, pairs, table, ghost, drag)
    returned = lax.ppermute(back, "gx", [(i + 1, i) for i in range(31)])
    head = pl.BlockSpec((3, 2048), lambda i: (0, 0))
    force, twist = call(
        border_kernel,
        (shape(3, 8192), shape(3, 8192)),
        [pl.BlockSpec((6, 16, 128), lambda i: (0, 0, 0)), head, head],
        outs=(head, head),
        grid=(1,),
        input_output_aliases={1: 0, 2: 1},
    )(returned, force, twist)
    pressure = call(pressure_kernel, shape(2, 8, 128), [VMEM_SPEC] * 2)(every, basis)
    return force, twist, pressure


def solution(mesh):
    return jax.shard_map(
        per_device,
        mesh=mesh,
        in_specs=(
            P(None, BOTH),
            P(None, BOTH),
            P(None, BOTH),
            P(BOTH),
            P(BOTH),
            P(BOTH, None, None),
            P(BOTH),
            P(None, "gx", "gy", None),
        ),
        out_specs=(P(None, BOTH), P(None, BOTH), P("gx", "gy", None)),
        check_vma=False,
    )
```

time: 962 us -> 69.4 us (0.07)
  the two profiles are of different devices: /device:TPU:1 before, /device:TPU:20 now
where the time goes in v1:
time: 69.4 us; the launch traced here: 68.6 us
  starting transfers between devices  34.3 us (49%)
  Pallas kernels  20.9 us (30%)
  waiting for transfers between devices  7.86 us (11%)
  local copies, waits for them, and re-layouts  4.07 us (6%)
  between operations  1.44 us (2%)
    pallas_call x1, Pallas kernels, per_device(): call(contact_kernel, (shape(3, 8192), shape(3, 8192), shape(6, 16, 128)),...  12.7 us
    all_to_all x1, starting transfers between devices, per_device(): every = lax.all_to_all(sums, BOTH, 0, 0, tiled=True)  8.45 us
    ppermute x1, starting transfers between devices, per_device(): side_b = lax.ppermute(wide, 'gx', odd_x)  7.74 us
    ppermute x1, starting transfers between devices, per_device(): returned = lax.ppermute(back, 'gx', [(i + 1, i) for i in range(31)])  6.44 us
    ppermute x1, waiting for transfers between devices, per_device(): far_c = lax.ppermute(side_a, 'gx', odd_x)  4.36 us
    unnamed x20, local copies, waits for them, and re-layouts  4.07 us
    ppermute x1, starting transfers between devices, per_device(): ghost = lax.ppermute(border, 'gx', [(i, i + 1) for i in range(31)])  3.89 us
    pallas_call x1, Pallas kernels, per_device(): call(deposit_kernel, (shape(4, 2, 8, 128), shape(3, 8192)), [VMEM_SPEC] * 4)  3.14 us
  transfers between devices with their start and end apart: 9, of which 3 were waited for; matrix products, arithmetic and copies ran while one was open for 0% of the time, Pallas kernels for 24%

profile of v1, /device:TPU:20, one launch (start us, length us, event | category | flops | bytes accessed | tf_op | source)
XLA Modules:
  0.0 68.6 jit_solution(6268833706579564121)
XLA Ops:
  0.6 0.0 copy-start
  0.6 0.9 %copy-done = f32[3,8192]{1,0:T(4,128)S(1)} copy-done((f32[3,8192]{1,0:T(4,128)S(1)}, f32[3,8192]{1,0:T(4,128)}, u32[]{:S(2)}) %copy-start) | copy-done | bytes 98328
  1.5 0.8 %copy-done.2 = f32[8192]{0:T(1024)S(1)} copy-done((f32[8192]{0:T(1024)S(1)}, f32[8192]{0:T(1024)}, u32[]{:S(2)}) %copy-start.2) | copy-done | bytes 32792
  2.3 0.8 %copy-done.4 = s32[8192]{0:T(1024)S(1)} copy-done((s32[8192]{0:T(1024)S(1)}, s32[8192]{0:T(1024)}, u32[]{:S(2)}) %copy-start.4) | copy-done | bytes 32792
  3.1 0.7 %copy-done.8 = f32[3,2,8,128]{3,2,1,0:T(8,128)S(1)} copy-done((f32[3,2,8,128]{3,2,1,0:T(8,128)S(1)}, f32[3,2,8,128]{3,2,1,0:T(8,128)}, u32[]{:S(2)}) %copy-start.8) | copy-done | bytes 24600
  3.8 3.1 %shard_map.104 = (f32[4,2,8,128]{3,2,1,0:T(8,128)S(1)}, f32[3,8192]{1,0:T(4,128)S(1)}) custom-call(f32[3,8192]{1,0:T(4,128)S(1)} %copy-done, f32[64,128]{1,0:T(8,128)S(1)} %bitcast.11, s32[64,128]{1,0:T(8,128)S(1)} %bitcast.13, f32[48,128]{1,0:T(8,128)S(1)} %bitcast.15), custom_call_target="tpu_custom_call" | custom-call | tf_op jit(solution)/shard_map/pallas_call | solution.py:386
  6.9 2.1 %collective-permute-start.3 = (f32[4,2,8,128]{3,2,1,0:T(8,128)S(1)}, f32[4,2,8,128]{3,2,1,0:T(8,128)S(1)}, u32[]{:S(2)}, u32[]{:S(2)}) collective-permute-start(f32[4,2,8,128]{3,2,1,0:T(8,128)S(1)} %get-tuple-element.22.own), channel_id=1, source_target_pairs={{1,2},{2,1},{3,4},{4,3},{5,6},{6,5},{9,10},{10,9},{11,12},{12,11},... | collective-permute-start | bytes 98312 | tf_op jit(solution)/shard_map/ppermute | solution.py:396
  9.0 1.5 %collective-permute-start.2 = (f32[4,2,8,128]{3,2,1,0:T(8,128)S(1)}, f32[4,2,8,128]{3,2,1,0:T(8,128)S(1)}, u32[]{:S(2)}, u32[]{:S(2)}) collective-permute-start(f32[4,2,8,128]{3,2,1,0:T(8,128)S(1)} %get-tuple-element.22.own), channel_id=1, source_target_pairs={{0,1},{1,0},{2,3},{3,2},{4,5},{5,4},{6,7},{7,6},{8,9},{9,8},{10,11... | collective-permute-start | bytes 98312 | tf_op jit(solution)/shard_map/ppermute | solution.py:395
  10.5 0.1 pad_add_fusion.place
  10.5 1.8 %collective-permute-done.3.odd_side = f32[4,2,8,128]{3,2,1,0:T(8,128)S(1)} collective-permute-done((f32[4,2,8,128]{3,2,1,0:T(8,128)S(1)}, f32[4,2,8,128]{3,2,1,0:T(8,128)S(1)}, u32[]{:S(2)}, u32[]{:S(2)}) %collective-permute-start.3) | collective-permute-done | bytes 32800 | tf_op jit(solution)/shard_map/ppermute | solution.py:396
  12.3 0.0 collective-permute-done.2.even_side
  12.3 0.6 shard_map.107.own
  12.9 7.7 %collective-permute-start.5 = (f32[3,2,16,128]{3,2,1,0:T(8,128)S(1)}, f32[3,2,16,128]{3,2,1,0:T(8,128)S(1)}, u32[]{:S(2)}, u32[]{:S(2)}) collective-permute-start(f32[3,2,16,128]{3,2,1,0:T(8,128)S(1)} %shard_map.107.own), channel_id=1, source_target_pairs={{8,16},{16,8},{24,32},{32,24},{40,48},{48,40},{56,64},{64,56},{72,... | collective-permute-start | bytes 147464 | tf_op jit(solution)/shard_map/ppermute | solution.py:402
  20.6 0.1 collective-permute-start.4
  20.8 0.0 copy-start.7
  20.8 0.9 %copy-done.7 = f32[3,8192]{1,0:T(4,128)S(1)} copy-done((f32[3,8192]{1,0:T(4,128)S(1)}, f32[3,8192]{1,0:T(4,128)}, u32[]{:S(2)}) %copy-start.7) | copy-done | bytes 98328
  21.7 0.7 %shard_map.103 = (bf16[320,512]{1,0:T(8,128)(2,1)S(1)}, f32[10,16,128]{2,1,0:T(8,128)S(1)}) custom-call(s32[2]{0:T(128)S(1)} %pad_add_fusion.place, f32[3,8192]{1,0:T(4,128)S(1)} %copy-done.6, f32[3,8192]{1,0:T(4,128)S(1)} %copy-done.1, f32[3,8192]{1,0:T(4,128)S(1)} %copy-done.7, f32[64,128]{1,0:T(8,128)S(1)} %bitcast.12, s32[64,128]{1,0:T(8,128)S(1)} %bitcast.14), custom_call_target="tpu_custom_call" | custom-call | tf_op jit(solution)/shard_map/pallas_call | solution.py:389
  22.4 3.9 %collective-permute-start = (f32[10,16,128]{2,1,0:T(8,128)S(1)}, f32[10,16,128]{2,1,0:T(8,128)S(1)}, u32[]{:S(2)}, u32[]{:S(2)}) collective-permute-start(f32[10,16,128]{2,1,0:T(8,128)S(1)} %get-tuple-element.15), channel_id=1, source_target_pairs={{0,8},{8,16},{16,24},{24,32},{32,40},{40,48},{48,56},{56,64},{64,7... | collective-permute-start | bytes 245768 | tf_op jit(solution)/shard_map/ppermute | solution.py:397
  26.3 0.0 collective-permute-done.5.side_b
  26.3 1.1 %collective-permute-start.7 = (f32[3,2,16,128]{3,2,1,0:T(8,128)S(1)}, f32[3,2,16,128]{3,2,1,0:T(8,128)S(1)}, u32[]{:S(2)}, u32[]{:S(2)}) collective-permute-start(f32[3,2,16,128]{3,2,1,0:T(8,128)S(1)} %collective-permute-done.5.side_b), channel_id=1, source_target_pairs={{0,8},{8,0},{16,24},{24,16},{32,40},{40,32},{48,56},{56,48},{64,72... | collective-permute-start | bytes 147464 | tf_op jit(solution)/shard_map/ppermute | solution.py:404
  27.4 0.0 collective-permute-done.4.side_a
  27.4 3.1 %collective-permute-start.6 = (f32[3,2,16,128]{3,2,1,0:T(8,128)S(1)}, f32[3,2,16,128]{3,2,1,0:T(8,128)S(1)}, u32[]{:S(2)}, u32[]{:S(2)}) collective-permute-start(f32[3,2,16,128]{3,2,1,0:T(8,128)S(1)} %collective-permute-done.4.side_a), channel_id=1, source_target_pairs={{8,16},{16,8},{24,32},{32,24},{40,48},{48,40},{56,64},{64,56},{72,... | collective-permute-start | bytes 147464 | tf_op jit(solution)/shard_map/ppermute | solution.py:403
  31.1 0.0 collective-permute-done.7.far_d
  31.1 4.4 %collective-permute-done.6.far_c = f32[3,2,16,128]{3,2,1,0:T(8,128)S(1)} collective-permute-done((f32[3,2,16,128]{3,2,1,0:T(8,128)S(1)}, f32[3,2,16,128]{3,2,1,0:T(8,128)S(1)}, u32[]{:S(2)}, u32[]{:S(2)}) %collective-permute-start.6) | collective-permute-done | bytes 49184 | tf_op jit(solution)/shard_map/ppermute | solution.py:403
  35.5 1.6 %shard_map.108 = (f32[256,128]{1,0:T(8,128)}, f32[3,2,8,128]{3,2,1,0:T(8,128)S(1)}) custom-call(s32[2]{0:T(128)S(1)} %pad_add_fusion.place, f32[3,2,16,128]{3,2,1,0:T(8,128)S(1)} %shard_map.107.own, f32[3,2,16,128]{3,2,1,0:T(8,128)S(1)} %collective-permute-done.4.side_a, f32[3,2,16,128]{3,2,1,0:T(8,128)S(1)} %collective-permute-done.5.side_b, ...), custom_call_target="tpu_custom_call" | custom-call | tf_op jit(solution)/shard_map/pallas_call | solution.py:405
  37.0 8.4 %all-to-all-start = ((f32[256,1,128]{2,1,0:T(1,128)}), f32[256,1,128]{2,1,0:T(1,128)S(1)}, u32[]{:S(2)}, u32[]{:S(2)}) async-start(f32[256,1,128]{2,1,0:T(1,128)} %bitcast.7), calls=%async_computation | async-start | bytes 262144 | tf_op jit(solution)/shard_map/all_to_all | solution.py:408
  45.5 0.0 collective-permute-done.ghost
  45.5 12.7 %shard_map.105 = (f32[3,8192]{1,0:T(4,128)}, f32[3,8192]{1,0:T(4,128)}, f32[6,16,128]{2,1,0:T(8,128)S(1)}) custom-call(s32[1]{0:T(128)S(6)} %copy.16.live, s32[128,128]{1,0:T(8,128)S(1)} %bitcast.16, bf16[320,512]{1,0:T(8,128)(2,1)S(1)} %get-tuple-element.14.table, f32[10,16,128]{2,1,0:T(8,128)S(1)} %collective-permute-done.ghost, ...), custom_call_target="tpu_custom_call" | custom-call | flops 5000000000 | bytes 1000000 | tf_op jit(solution)/shard_map/pallas_call | solution.py:410
  58.2 6.4 %collective-permute-start.1 = (f32[6,16,128]{2,1,0:T(8,128)S(1)}, f32[6,16,128]{2,1,0:T(8,128)S(1)}, u32[]{:S(2)}, u32[]{:S(2)}) collective-permute-start(f32[6,16,128]{2,1,0:T(8,128)S(1)} %get-tuple-element.17), channel_id=1, source_target_pairs={{8,0},{16,8},{24,16},{32,24},{40,32},{48,40},{56,48},{64,56},{72,6... | collective-permute-start | bytes 147464 | tf_op jit(solution)/shard_map/ppermute | solution.py:417
  64.7 1.7 %collective-permute-done.1.returned = f32[6,16,128]{2,1,0:T(8,128)S(1)} collective-permute-done((f32[6,16,128]{2,1,0:T(8,128)S(1)}, f32[6,16,128]{2,1,0:T(8,128)S(1)}, u32[]{:S(2)}, u32[]{:S(2)}) %collective-permute-start.1) | collective-permute-done | bytes 49184 | tf_op jit(solution)/shard_map/ppermute | solution.py:417
  66.4 1.5 %shard_map.106 = (f32[3,8192]{1,0:T(4,128)}, f32[3,8192]{1,0:T(4,128)}) custom-call(f32[6,16,128]{2,1,0:T(8,128)S(1)} %collective-permute-done.1.returned, f32[3,8192]{1,0:T(4,128)} %get-tuple-element.18.force_in, f32[3,8192]{1,0:T(4,128)} %get-tuple-element.19.twist_in), custom_call_target="tpu_custom_call", output_to_operand_aliasing={{0}: (1, {}), {1}: (2, {})} | custom-call | tf_op jit(solution)/shard_map/pallas_call | solution.py:419
  67.8 0.7 %shard_map.109 = f32[2,8,128]{2,1,0:T(8,128)} custom-call(f32[256,128]{1,0:T(8,128)S(1)} %bitcast.10, f32[3,2,8,128]{3,2,1,0:T(8,128)S(1)} %get-tuple-element.24.basis), custom_call_target="tpu_custom_call" | custom-call | tf_op jit(solution)/shard_map/pallas_call | solution.py:427
  (14 shorter events, 0.0 us)
Async XLA Ops:
  0.6 0.9 %copy-start = (f32[3,8192]{1,0:T(4,128)S(1)}, f32[3,8192]{1,0:T(4,128)}, u32[]{:S(2)}) copy-start(f32[3,8192]{1,0:T(4,128)} %vel.3) | copy-start | bytes 294916
  1.5 0.8 %copy-start.2 = (f32[8192]{0:T(1024)S(1)}, f32[8192]{0:T(1024)}, u32[]{:S(2)}) copy-start(f32[8192]{0:T(1024)} %param.11) | copy-start | bytes 98308
  2.3 0.8 %copy-start.4 = (s32[8192]{0:T(1024)S(1)}, s32[8192]{0:T(1024)}, u32[]{:S(2)}) copy-start(s32[8192]{0:T(1024)} %param.12) | copy-start | bytes 98308
  3.1 0.7 %copy-start.8 = (f32[3,2,8,128]{3,2,1,0:T(8,128)S(1)}, f32[3,2,8,128]{3,2,1,0:T(8,128)}, u32[]{:S(2)}) copy-start(f32[3,2,8,128]{3,2,1,0:T(8,128)} %param.15) | copy-start | bytes 73732
  3.8 16.9 %copy-start.5 = (s32[8192]{0:T(1024)S(1)}, s32[8192]{0:T(1024)}, u32[]{:S(2)}) copy-start(s32[8192]{0:T(1024)} %param.12) | copy-start | bytes 98308
  3.8 16.9 %copy-start.6 = (f32[3,8192]{1,0:T(4,128)S(1)}, f32[3,8192]{1,0:T(4,128)}, u32[]{:S(2)}) copy-start(f32[3,8192]{1,0:T(4,128)} %pos.1) | copy-start | bytes 294916
  6.9 13.8 %copy-start.1 = (f32[3,8192]{1,0:T(4,128)S(1)}, f32[3,8192]{1,0:T(4,128)}, u32[]{:S(2)}) copy-start(f32[3,8192]{1,0:T(4,128)} %vel.3) | copy-start | bytes 294916
  6.9 5.4 %collective-permute-start.3 = (f32[4,2,8,128]{3,2,1,0:T(8,128)S(1)}, f32[4,2,8,128]{3,2,1,0:T(8,128)S(1)}, u32[]{:S(2)}, u32[]{:S(2)}) collective-permute-start(f32[4,2,8,128]{3,2,1,0:T(8,128)S(1)} %get-tuple-element.22.own), channel_id=1, source_target_pairs={{1,2},{2,1},{3,4},{4,3},{5,6},{6,5},{9,10},{10,9},{11,12},{12,11},... | collective-permute-start | bytes 98312 | tf_op jit(solution)/shard_map/ppermute | solution.py:396
  9.0 3.3 %collective-permute-start.2 = (f32[4,2,8,128]{3,2,1,0:T(8,128)S(1)}, f32[4,2,8,128]{3,2,1,0:T(8,128)S(1)}, u32[]{:S(2)}, u32[]{:S(2)}) collective-permute-start(f32[4,2,8,128]{3,2,1,0:T(8,128)S(1)} %get-tuple-element.22.own), channel_id=1, source_target_pairs={{0,1},{1,0},{2,3},{3,2},{4,5},{5,4},{6,7},{7,6},{8,9},{9,8},{10,11... | collective-permute-start | bytes 98312 | tf_op jit(solution)/shard_map/ppermute | solution.py:395
  10.5 10.2 %copy-start.3 = (f32[8192]{0:T(1024)S(1)}, f32[8192]{0:T(1024)}, u32[]{:S(2)}) copy-start(f32[8192]{0:T(1024)} %param.11) | copy-start | bytes 98308
  12.9 13.4 %collective-permute-start.5 = (f32[3,2,16,128]{3,2,1,0:T(8,128)S(1)}, f32[3,2,16,128]{3,2,1,0:T(8,128)S(1)}, u32[]{:S(2)}, u32[]{:S(2)}) collective-permute-start(f32[3,2,16,128]{3,2,1,0:T(8,128)S(1)} %shard_map.107.own), channel_id=1, source_target_pairs={{8,16},{16,8},{24,32},{32,24},{40,48},{48,40},{56,64},{64,56},{72,... | collective-permute-start | bytes 147464 | tf_op jit(solution)/shard_map/ppermute | solution.py:402
  20.6 6.8 %collective-permute-start.4 = (f32[3,2,16,128]{3,2,1,0:T(8,128)S(1)}, f32[3,2,16,128]{3,2,1,0:T(8,128)S(1)}, u32[]{:S(2)}, u32[]{:S(2)}) collective-permute-start(f32[3,2,16,128]{3,2,1,0:T(8,128)S(1)} %shard_map.107.own), channel_id=1, source_target_pairs={{0,8},{8,0},{16,24},{24,16},{32,40},{40,32},{48,56},{56,48},{64,72... | collective-permute-start | bytes 147464 | tf_op jit(solution)/shard_map/ppermute | solution.py:401
  20.8 0.9 %copy-start.7 = (f32[3,8192]{1,0:T(4,128)S(1)}, f32[3,8192]{1,0:T(4,128)}, u32[]{:S(2)}) copy-start(f32[3,8192]{1,0:T(4,128)} %spin.1) | copy-start | bytes 294916
  22.4 23.1 %collective-permute-start = (f32[10,16,128]{2,1,0:T(8,128)S(1)}, f32[10,16,128]{2,1,0:T(8,128)S(1)}, u32[]{:S(2)}, u32[]{:S(2)}) collective-permute-start(f32[10,16,128]{2,1,0:T(8,128)S(1)} %get-tuple-element.15), channel_id=1, source_target_pairs={{0,8},{8,16},{16,24},{24,32},{32,40},{40,48},{48,56},{56,64},{64,7... | collective-permute-start | bytes 245768 | tf_op jit(solution)/shard_map/ppermute | solution.py:397
  26.3 4.8 %collective-permute-start.7 = (f32[3,2,16,128]{3,2,1,0:T(8,128)S(1)}, f32[3,2,16,128]{3,2,1,0:T(8,128)S(1)}, u32[]{:S(2)}, u32[]{:S(2)}) collective-permute-start(f32[3,2,16,128]{3,2,1,0:T(8,128)S(1)} %collective-permute-done.5.side_b), channel_id=1, source_target_pairs={{0,8},{8,0},{16,24},{24,16},{32,40},{40,32},{48,56},{56,48},{64,72... | collective-permute-start | bytes 147464 | tf_op jit(solution)/shard_map/ppermute | solution.py:404
  27.4 8.1 %collective-permute-start.6 = (f32[3,2,16,128]{3,2,1,0:T(8,128)S(1)}, f32[3,2,16,128]{3,2,1,0:T(8,128)S(1)}, u32[]{:S(2)}, u32[]{:S(2)}) collective-permute-start(f32[3,2,16,128]{3,2,1,0:T(8,128)S(1)} %collective-permute-done.4.side_a), channel_id=1, source_target_pairs={{8,16},{16,8},{24,32},{32,24},{40,48},{48,40},{56,64},{64,56},{72,... | collective-permute-start | bytes 147464 | tf_op jit(solution)/shard_map/ppermute | solution.py:403
  37.0 8.5 %copy-start.9 = (s32[64,2,128]{2,1,0:T(2,128)S(1)}, s32[64,2,128]{2,1,0:T(2,128)}, u32[]{:S(2)}) copy-start(s32[64,2,128]{2,1,0:T(2,128)} %param.13) | copy-start | bytes 196612
  37.0 30.8 %all-to-all-start = ((f32[256,1,128]{2,1,0:T(1,128)}), f32[256,1,128]{2,1,0:T(1,128)S(1)}, u32[]{:S(2)}, u32[]{:S(2)}) async-start(f32[256,1,128]{2,1,0:T(1,128)} %bitcast.7), calls=%async_computation | async-start | bytes 262144 | tf_op jit(solution)/shard_map/all_to_all | solution.py:408
  58.2 8.2 %collective-permute-start.1 = (f32[6,16,128]{2,1,0:T(8,128)S(1)}, f32[6,16,128]{2,1,0:T(8,128)S(1)}, u32[]{:S(2)}, u32[]{:S(2)}) collective-permute-start(f32[6,16,128]{2,1,0:T(8,128)S(1)} %get-tuple-element.17), channel_id=1, source_target_pairs={{8,0},{16,8},{24,16},{32,24},{40,32},{48,40},{56,48},{64,56},{72,6... | collective-permute-start | bytes 147464 | tf_op jit(solution)/shard_map/ppermute | solution.py:417

commit v2 on v1

v2 whole, which is shorter than its diff:
```python
import functools

import jax
import jax.numpy as jnp
from jax import lax
from jax.experimental import pallas as pl
from jax.experimental.pallas import tpu as pltpu
from jax.sharding import PartitionSpec as P

STIFFNESS = 4.0
DAMPING = 1.0
FRICTION = 0.5
SLIP_SCALE = 0.1
DRAG_RATE = 3.0
SPHERE = 4.18879020478639

F32 = jnp.float32
BF16 = jnp.bfloat16
BOTH = ("gx", "gy")
VMEM_SPEC = pl.BlockSpec(memory_space=pltpu.VMEM)
SMEM_SPEC = pl.BlockSpec(memory_space=pltpu.SMEM)
PARAMS = pltpu.CompilerParams(vmem_limit_bytes=24 * 1024 * 1024)


def split(x):
    high = x.astype(BF16)
    return high, (x - high.astype(F32)).astype(BF16)


def one_hot(size, index):
    rows = lax.broadcasted_iota(jnp.int32, (size, index.shape[1]), 0)
    return rows == index


def hot_rows(size, index):
    rows = lax.broadcasted_iota(jnp.int32, (size, 128), 0).astype(F32).astype(BF16)
    out = []
    for k in range(index.shape[1] // 128):
        here = index[:, 128 * k : 128 * k + 128].astype(F32)
        here = jnp.broadcast_to(here, (size, 128)).astype(BF16)
        out.append(jnp.where(rows == here, jnp.ones((), BF16), jnp.zeros((), BF16)))
    return jnp.concatenate(out, axis=1)


def as_bf16(mask):
    return jnp.where(mask, 1.0, 0.0).astype(BF16)


def lanes(block, rows):
    return jnp.concatenate([block[r : r + 1, :] for r in rows], axis=1)


def dot_nt(left, right):
    return lax.dot_general(left, right, (((1,), (1,)), ((), ())), preferred_element_type=F32)


def fold(blocks):
    sub = lax.broadcasted_iota(jnp.int32, (8, 128), 0)
    for step in (4, 2, 1):
        low = (sub & step) == 0
        half = len(blocks) // 2
        blocks = [
            jnp.where(
                low,
                blocks[i] + pltpu.roll(blocks[i], 8 - step, 0),
                blocks[i + half] + pltpu.roll(blocks[i + half], step, 0),
            )
            for i in range(half)
        ]
    return blocks[0]


def tiles(x):
    return [x[:, 128 * k : 128 * k + 128] for k in range(x.shape[1] // 128)]


def halves(x):
    high = x.astype(BF16).astype(F32)
    return high, (x - high).astype(BF16).astype(F32)


def dense(ref, d, count=64):
    return jnp.concatenate(
        [ref[d : d + 1, 128 * k : 128 * k + 128] for k in range(count)], axis=0
    )


def spread(ref, v, row, masks):
    value = jnp.broadcast_to(ref[v, pl.ds(row, 1), :], (16, 128)).astype(BF16)
    return [value * m for m in masks]


def load_all(sources, targets, sems):
    copies = [
        pltpu.make_async_copy(src, dst, sems.at[k])
        for k, (src, dst) in enumerate(zip(sources, targets))
    ]
    for copy in copies:
        copy.start()
    return copies


def deposit_kernel(
    cell_in, fluid_in, radius_in, vel_in, pos_in, spin_in,
    fields, drag, cell, radius, vel, pos, spin, fluid, parts, sems,
):
    copies = load_all(
        (cell_in, fluid_in, radius_in, vel_in, pos_in, spin_in),
        (cell, fluid, radius, vel, pos, spin),
        sems,
    )
    for copy in copies[:4]:
        copy.wait()
    fluid_high, fluid_low = split(fluid[...])
    fluid_table = jnp.concatenate([fluid_high, fluid_low], axis=1)
    total = jnp.zeros((128, 128), F32)
    for g in range(8):
        rows = slice(8 * g, 8 * g + 8)
        cells = lanes(cell[rows, :], range(8))
        hot = hot_rows(128, cells & 127)
        mask = one_hot(16, cells >> 7)
        seen = jnp.dot(
            fluid_table, jnp.concatenate([hot, hot], axis=0), preferred_element_type=F32
        )
        rad = radius[rows, :]
        values = []
        for d in range(3):
            chosen = jnp.where(mask, seen[16 * d : 16 * d + 16], 0.0)
            u = fold(tiles(chosen[0:8] + chosen[8:16]))
            v = jnp.concatenate(
                [vel[d : d + 1, 1024 * g + 128 * k : 1024 * g + 128 * k + 128] for k in range(8)],
                axis=0,
            )
            force = DRAG_RATE * rad * (u - v)
            drag[d, rows, :] = force
            values.append(-force)
        values.append(SPHERE * rad * rad * rad)
        for k, value in enumerate(values):
            high, low = halves(value)
            parts[k, rows, :] = high
            parts[4 + k, rows, :] = low
        masks = tiles(as_bf16(mask))
        left = [
            jnp.concatenate([spread(parts, v, 8 * g + k, masks[k : k + 1])[0] for v in range(8)], 0)
            for k in range(8)
        ]
        total = total + dot_nt(jnp.concatenate(left, axis=1), hot)
    total = total[0:64] + total[64:128]
    lane = lax.broadcasted_iota(jnp.int32, (16, 128), 1)
    mz = total[32:48]
    up = jnp.where(lane == 127, 0.0, pltpu.roll(mz, 127, 1))
    down = jnp.where(lane == 0, 0.0, pltpu.roll(mz, 1, 1))
    out = [total[0:16], 1.0 / (1.0 + total[48:64]), total[16:32], 0.5 * (up - down)]
    for f in range(4):
        for layer in range(2):
            fields[f, layer] = out[f][8 * layer : 8 * layer + 8]
    for copy in copies[4:]:
        copy.wait()


def table_kernel(place, pos, vel, spin, radius, cell, table, border):
    cells = cell[...]
    rad = radius[...]
    corner = [
        place[0] * 2 + (cells >> 10),
        place[1] * 8 + ((cells >> 7) & 7),
        cells & 127,
    ]
    fields = [dense(pos, d) - corner[d].astype(F32) for d in range(3)]
    fields += [dense(vel, d) for d in range(3)]
    fields += [rad * dense(spin, d) for d in range(3)]
    fields += [rad]
    for f in range(10):
        high, low = split(fields[f])
        rows = pl.ds(32 * f, 32)
        table[rows, 0:128] = high[0:32]
        table[rows, 128:256] = high[32:64]
        table[rows, 256:384] = low[0:32]
        table[rows, 384:512] = low[32:64]
        border[f] = fields[f][0:16] - 1.0 if f == 0 else fields[f][0:16]


BLOCKS = 32


def first_index(block):
    index = lanes(block, range(0, 16, 2))
    return (index >> 7) & 31, (index & 127) + ((index >> 12) << 7)


def second_index(block):
    index = lanes(block, range(1, 16, 2))
    beyond = index - 8192
    row = jnp.where(beyond >= 0, 32 + ((beyond >> 7) & 7), (index >> 7) & 31)
    side = jnp.where(beyond >= 0, beyond >> 10, index >> 12)
    return row, (index & 127) + (side << 7)


def groups(live):
    return (jnp.minimum(live, BLOCKS) + 7) // 8


def pair_block(pairs, it):
    return pairs[pl.ds(pl.multiple_of(it * 16, 16), 16), :]


def gather(table, row, place, beyond):
    out = [[] for _ in range(10)]
    for part in range(2):
        here = slice(512 * part, 512 * part + 512)
        hot = hot_rows(256, place[:, here])
        mask = one_hot(32, row[:, here])
        seen = jnp.dot(table[...], jnp.concatenate([hot, hot], axis=0), preferred_element_type=F32)
        for f in range(10):
            s = jnp.where(mask, seen[32 * f : 32 * f + 32], 0.0)
            s = (s[0:8] + s[8:16]) + (s[16:24] + s[24:32])
            if beyond:
                mask_far = one_hot(8, row[:, here] - 32)
                s = s + jnp.where(mask_far, seen[320 + 8 * f : 328 + 8 * f], 0.0)
            out[f] += tiles(s)
    return [fold(x) for x in out]


def cross(a, b):
    return [
        a[1] * b[2] - a[2] * b[1],
        a[2] * b[0] - a[0] * b[2],
        a[0] * b[1] - a[1] * b[0],
    ]


def dot3(a, b):
    return a[0] * b[0] + a[1] * b[1] + a[2] * b[2]


def contact_terms(first, second):
    offset = [second[d] - first[d] for d in range(3)]
    distance = jnp.sqrt(dot3(offset, offset))
    reach = first[9] + second[9]
    inverse = 1.0 / jnp.maximum(distance, 0.25 * reach)
    normal = [o * inverse for o in offset]
    correlation = jnp.maximum(reach - distance, 0.0)
    root = jnp.sqrt(correlation)
    lever = [first[6 + d] + second[6 + d] for d in range(3)]
    turn = cross(lever, normal)
    slip = [second[3 + d] - first[3 + d] - turn[d] for d in range(3)]
    speed = dot3(slip, normal)
    push = STIFFNESS * correlation * root - DAMPING * root * speed
    tangent = [slip[d] - speed * normal[d] for d in range(3)]
    size = jnp.sqrt(dot3(tangent, tangent) + SLIP_SCALE * SLIP_SCALE)
    scale = FRICTION * jnp.abs(push) / size
    friction = [scale * t for t in tangent]
    force = [friction[d] - push * normal[d] for d in range(3)]
    twist = cross(normal, friction)
    return force, twist


def contact_kernel(live, pairs, table, ghost, parts_p, parts_q, back, first, second, full, sum_far):
    count = live[0]
    full[0:320, :] = table[...]
    pieces = [
        jnp.concatenate([ghost[f, 0:8, :], ghost[f, 8:16, :]], axis=1) for f in range(10)
    ]
    high, low = split(jnp.concatenate(pieces, axis=0))
    full[320:400, 0:256] = high
    full[320:400, 256:512] = low

    def look(it, carry):
        block = pair_block(pairs, it)
        rows = pl.ds(pl.multiple_of(it * 8, 8), 8)
        p = gather(table, *first_index(block), False)
        q = gather(full, *second_index(block), True)
        for f in range(10):
            first[f, rows, :] = p[f]
            second[f, rows, :] = q[f]
        return carry

    lax.fori_loop(0, groups(count), look, 0)
    p = [first[f] for f in range(10)]
    q = [second[f] for f in range(10)]
    force, twist = contact_terms(p, q)
    keep = lax.broadcasted_iota(jnp.int32, (BLOCKS, 128), 0) < count
    to_p = force + [p[9] * v for v in twist]
    to_q = [-v for v in force] + [q[9] * v for v in twist]
    for k in range(6):
        for parts, values in ((parts_p, to_p), (parts_q, to_q)):
            high, low = halves(jnp.where(keep, values[k], 0.0))
            parts[k] = high
            parts[6 + k] = low
    sum_far[...] = jnp.zeros_like(sum_far)

    def step(it, carry):
        row, place = second_index(pair_block(pairs, it))
        hot = hot_rows(256, place)
        far = as_bf16(one_hot(16, row - 32))
        left = [
            jnp.concatenate(
                sum([spread(parts_q, v, it * 8 + k, [m]) for v in range(12)], []), axis=0
            )
            for k, m in enumerate(tiles(far))
        ]
        sum_far[...] += dot_nt(jnp.concatenate(left, axis=1), hot)
        return carry

    lax.fori_loop(0, groups(count), step, 0)
    for f in range(6):
        rows = sum_far[16 * f : 16 * f + 8, :] + sum_far[96 + 16 * f : 104 + 16 * f, :]
        back[f, 0:8, :] = rows[:, 0:128]
        back[f, 8:16, :] = rows[:, 128:256]


def own_kernel(live, pairs, parts_p, parts_q, total, sum_p, sum_q):
    sum_p[...] = jnp.zeros_like(sum_p)
    sum_q[...] = jnp.zeros_like(sum_q)

    def step(it, carry):
        block = pair_block(pairs, it)
        for index, parts, sums in (
            (first_index, parts_p, sum_p),
            (second_index, parts_q, sum_q),
        ):
            row, place = index(block)
            hot = hot_rows(256, place)
            mask = as_bf16(one_hot(32, row))
            left = [
                jnp.concatenate(
                    sum([spread(parts, v, it * 8 + k, [m[0:16], m[16:32]]) for v in range(12)], []),
                    axis=0,
                )
                for k, m in enumerate(tiles(mask))
            ]
            sums[...] += dot_nt(jnp.concatenate(left, axis=1), hot)
        return carry

    lax.fori_loop(0, groups(live[0]), step, 0)
    for f in range(6):
        rows = slice(32 * f, 32 * f + 32)
        rest = slice(192 + 32 * f, 224 + 32 * f)
        own = (sum_p[rows, :] + sum_p[rest, :]) + (sum_q[rows, :] + sum_q[rest, :])
        total[f, 0:32, :] = own[:, 0:128]
        total[f, 32:64, :] = own[:, 128:256]


def finish_kernel(total, returned, drag, sums, basis, force_out, twist_out, pressure):
    solve(sums, basis, pressure)
    for f in range(3):
        for g in range(8):
            rows = slice(8 * g, 8 * g + 8)
            force = total[f, rows, :] + drag[f, rows, :]
            twist = total[3 + f, rows, :]
            if g < 2:
                force = force + returned[f, rows, :]
                twist = twist + returned[3 + f, rows, :]
            for k in range(8):
                at = slice(1024 * g + 128 * k, 1024 * g + 128 * k + 128)
                force_out[f : f + 1, at] = force[k : k + 1]
                twist_out[f : f + 1, at] = twist[k : k + 1]


def next_row(x):
    return pltpu.roll(x, x.shape[0] - 1, 0)


def last_row(x):
    return pltpu.roll(x, 1, 0)


def rows_kernel(place, own, even_side, odd_side, near, slim):
    even = (place[1] & 1) == 0
    sub = lax.broadcasted_iota(jnp.int32, (8, 128), 0)

    def extend(f, layer):
        e, o = even_side[f, layer], odd_side[f, layer]
        after = jnp.where(even, e, o)
        before = jnp.where(even, o, e)
        return jnp.concatenate([own[f, layer], jnp.where(sub < 4, after, before)], axis=0)

    def put(f, layer, x):
        near[32 * f + 16 * layer : 32 * f + 16 * layer + 16, :] = x

    for layer in range(2):
        mx = extend(0, layer)
        my = extend(2, layer)
        part = extend(3, layer) + 0.5 * (next_row(my) - last_row(my))
        put(0, layer, mx)
        put(1, layer, extend(1, layer))
        put(2, layer, part)
        slim[0, layer] = mx[0:8]
        slim[1, layer] = mx[8:16]
        slim[2, layer] = own[1, layer]
        slim[3, layer] = part[0:8]


SHIFT = 3.0


def krylov_kernel(place, own, near_a, near_b, far_a, far_b, sums, basis):
    gx, gy = place[0], place[1]
    up_a = (gx & 1) == 0
    far_up_a = (gx & 2) == 0
    blank = jnp.zeros((8, 128), F32)

    def layers(f):
        def far(ref, s):
            if f == 0:
                return jnp.concatenate([ref[0, s], ref[1, s]], axis=0)
            return jnp.concatenate([ref[1 + f, s], blank], axis=0)

        pick = lambda cond, u, v: [jnp.where(cond, x, y) for x, y in zip(u, v)]
        near = lambda ref, s: ref[32 * f + 16 * s : 32 * f + 16 * s + 16, :]
        a = [near(near_a, s) for s in range(2)]
        b = [near(near_b, s) for s in range(2)]
        c = [far(far_a, s) for s in range(2)]
        d = [far(far_b, s) for s in range(2)]
        return (
            pick(far_up_a, d, c)
            + pick(up_a, b, a)
            + [near(own, 0), near(own, 1)]
            + pick(up_a, a, b)
            + pick(far_up_a, c, d)
        )

    mx, por, part = layers(0), layers(1), layers(2)
    row = lax.broadcasted_iota(jnp.int32, (16, 128), 0)
    lane = lax.broadcasted_iota(jnp.int32, (16, 128), 1)
    inside_y = (row < 8) | ((row < 12) & (gy < 7)) | ((row >= 12) & (gy > 0))

    def inside(l):
        x = gx * 2 + (l - 4)
        return inside_y & (x >= 0) & (x < 64)

    masks = [inside(l) for l in range(10)]
    zplus = lambda x: jnp.where(lane == 127, 0.0, pltpu.roll(x, 127, 1))
    zminus = lambda x: jnp.where(lane == 0, 0.0, pltpu.roll(x, 1, 1))
    half = [0.5 * p for p in por]
    wx = [half[l] + half[l + 1] for l in range(9)]
    wy = [h + next_row(h) for h in half]
    wy_low = [last_row(w) for w in wy]
    wz = [h + zplus(h) for h in half]
    wz_low = [h + zminus(h) for h in half]

    def apply(p, l):
        c = p[l]
        return (
            wx[l] * (c - p[l + 1])
            + wx[l - 1] * (c - p[l - 1])
            + wy[l] * (c - next_row(c))
            + wy_low[l] * (c - last_row(c))
            + wz[l] * (c - zplus(c))
            + wz_low[l] * (c - zminus(c))
        )

    v0 = {
        l: jnp.where(masks[l], part[l] + 0.5 * (mx[l + 1] - mx[l - 1]), 0.0) for l in range(1, 9)
    }
    a0 = {l: apply(v0, l) for l in range(2, 8)}
    v1 = {l: jnp.where(masks[l], a0[l] * (1.0 / SHIFT) - v0[l], 0.0) for l in a0}
    a1 = {l: apply(v1, l) for l in range(3, 7)}
    v2 = {l: jnp.where(masks[l], a1[l] * (1.0 / SHIFT) - v1[l], 0.0) for l in a1}
    a2 = {l: apply(v2, l) for l in range(4, 6)}

    def inner(p, q):
        return p[4][0:8] * q[4][0:8] + p[5][0:8] * q[5][0:8]

    products = [
        inner(v0, a0),
        inner(v1, a0),
        inner(v2, a0),
        inner(v1, a1),
        inner(v2, a1),
        inner(v2, a2),
        inner(v0, v0),
        inner(v1, v0),
    ]
    at = lax.broadcasted_iota(jnp.int32, (8, 128), 1)
    sub = lax.broadcasted_iota(jnp.int32, (8, 128), 0)
    eight = jnp.sum(fold(products), axis=1, keepdims=True)
    ninth = jnp.sum(inner(v2, v0), keepdims=True)
    line = jnp.sum(jnp.where(at == sub, eight, 0.0), axis=0, keepdims=True)
    line = line + jnp.where(at[0:1] == 8, ninth, 0.0)
    sums[...] = jnp.broadcast_to(line, (256, 128))
    for s in range(2):
        basis[0, s] = v0[4 + s][0:8]
        basis[1, s] = v1[4 + s][0:8]
        basis[2, s] = v2[4 + s][0:8]


def solve(sums, basis, pressure):
    line = jnp.sum(sums[...], axis=0, keepdims=True)
    at = lax.broadcasted_iota(jnp.int32, (1, 128), 1)
    h00, h01, h02, h11, h12, h22, g0, g1, g2 = [
        jnp.sum(jnp.where(at == k, line, 0.0), axis=1, keepdims=True) for k in range(9)
    ]
    l10 = h01 / h00
    l20 = h02 / h00
    d1 = h11 - l10 * h01
    e = h12 - l10 * h02
    l21 = e / d1
    d2 = h22 - l20 * h02 - l21 * e
    y1 = g1 - l10 * g0
    y2 = g2 - l20 * g0 - l21 * y1
    c2 = y2 / d2
    c1 = y1 / d1 - l21 * c2
    c0 = g0 / h00 - l10 * c1 - l20 * c2
    for s in range(2):
        pressure[s] = c0 * basis[0, s] + c1 * basis[1, s] + c2 * basis[2, s]


def shape(*dims, dtype=F32):
    return jax.ShapeDtypeStruct(dims, dtype)


def call(kernel, out, specs, outs=None, scratch=(), cost=None, **more):
    return pl.pallas_call(
        kernel,
        out_shape=out,
        in_specs=specs,
        out_specs=outs if outs is not None else jax.tree.map(lambda _: VMEM_SPEC, out),
        scratch_shapes=scratch,
        compiler_params=PARAMS,
        cost_estimate=cost,
        **more,
    )


def work(us):
    return pl.CostEstimate(flops=us * 10**9, bytes_accessed=0, transcendentals=0)


def in_hbm(*arrays):
    return [pltpu.with_memory_space_constraint(x, pltpu.HBM) for x in arrays]


def swaps(count):
    even = [(i, i ^ 1) for i in range(count)]
    odd = [(i, ((i + 1) ^ 1) - 1) for i in range(1, count - 1)]
    return even, odd


def per_device(pos, vel, spin, radius, cell, pairs, live, fluid):
    place = jnp.stack([lax.axis_index("gx"), lax.axis_index("gy")]).astype(jnp.int32)
    radius = radius.reshape(64, 128)
    cell = cell.reshape(64, 128)
    pairs = pairs.reshape(128, 128)
    fluid = fluid.reshape(48, 128)
    even_x, odd_x = swaps(32)
    even_y, odd_y = swaps(8)

    hbm = pl.BlockSpec(memory_space=pltpu.HBM)
    flat = shape(64, 128)
    fields, drag, cell, radius, vel, pos, spin = call(
        deposit_kernel,
        (
            shape(4, 2, 8, 128),
            shape(3, 64, 128),
            shape(64, 128, dtype=jnp.int32),
            flat,
            shape(3, 8192),
            shape(3, 8192),
            shape(3, 8192),
        ),
        [hbm] * 6,
        scratch=[
            pltpu.VMEM((48, 128), F32),
            pltpu.VMEM((8, 64, 128), F32),
            pltpu.SemaphoreType.DMA((6,)),
        ],
    )(*in_hbm(cell, fluid, radius, vel, pos, spin))
    table, border = call(
        table_kernel,
        (shape(320, 512, dtype=BF16), shape(10, 16, 128)),
        [SMEM_SPEC] + [VMEM_SPEC] * 5,
    )(place, pos, vel, spin, radius, cell)

    even_side = lax.ppermute(fields, "gy", even_y)
    odd_side = lax.ppermute(fields, "gy", odd_y)
    near, slim = call(
        rows_kernel,
        (shape(96, 128), shape(4, 2, 8, 128)),
        [SMEM_SPEC] + [VMEM_SPEC] * 3,
    )(place, fields, even_side, odd_side)
    near, slim, border = lax.optimization_barrier((near, slim, border))
    near_b = lax.ppermute(near, "gx", odd_x)
    far_b = lax.ppermute(slim, "gx", [(i, ((i + 2) ^ 2) - 2) for i in range(2, 30)])
    near_a = lax.ppermute(near, "gx", even_x)
    far_a = lax.ppermute(slim, "gx", [(i, i ^ 2) for i in range(32)])
    ghost = lax.ppermute(border, "gx", [(i, i + 1) for i in range(31)])
    sums, basis = call(
        krylov_kernel, (shape(256, 128), shape(3, 2, 8, 128)), [SMEM_SPEC] + [VMEM_SPEC] * 5, cost=work(8),
    )(place, near, near_a, near_b, far_a, far_b)
    every = lax.all_to_all(sums, BOTH, 0, 0, tiled=True)

    table, sums = lax.optimization_barrier((table, sums))
    sums_384 = pltpu.VMEM((384, 256), F32)
    found = pltpu.VMEM((10, BLOCKS, 128), F32)
    twelve = shape(12, BLOCKS, 128)
    parts_p, parts_q, back = call(
        contact_kernel,
        (twelve, twelve, shape(6, 16, 128)),
        [SMEM_SPEC] + [VMEM_SPEC] * 3,
        scratch=[found, found, pltpu.VMEM((400, 512), BF16), pltpu.VMEM((192, 256), F32)],
        cost=work(2),
    )(live, pairs, table, ghost)
    returned = lax.ppermute(back, "gx", [(i + 1, i) for i in range(31)])
    total = call(
        own_kernel,
        shape(6, 64, 128),
        [SMEM_SPEC] + [VMEM_SPEC] * 3,
        scratch=[sums_384, sums_384],
        cost=work(1),
    )(live, pairs, parts_p, parts_q)
    return call(
        finish_kernel,
        (shape(3, 8192), shape(3, 8192), shape(2, 8, 128)),
        [VMEM_SPEC] * 5,
    )(total, returned, drag, every, basis)


def solution(mesh):
    return jax.shard_map(
        per_device,
        mesh=mesh,
        in_specs=(
            P(None, BOTH),
            P(None, BOTH),
            P(None, BOTH),
            P(BOTH),
            P(BOTH),
            P(BOTH, None, None),
            P(BOTH),
            P(None, "gx", "gy", None),
        ),
        out_specs=(P(None, BOTH), P(None, BOTH), P("gx", "gy", None)),
        check_vma=False,
    )
```

time: 69.4 us -> 55.5 us (0.80)
  the two profiles are of different devices: /device:TPU:20 before, /device:TPU:1 now
where the time goes in v2:
time: 55.5 us; the launch traced here: 54.7 us
  starting transfers between devices  34.7 us (63%)
  Pallas kernels  12.4 us (22%)
  waiting for transfers between devices  6.1 us (11%)
  between operations  1.43 us (3%)
    all_to_all x1, starting transfers between devices, per_device(): every = lax.all_to_all(sums, BOTH, 0, 0, tiled=True)  14.1 us
    ppermute x1, starting transfers between devices, per_device(): far_a = lax.ppermute(slim, 'gx', [(i, i ^ 2) for i in range(32)])  6.73 us
    ppermute x1, starting transfers between devices, per_device(): near_a = lax.ppermute(near, 'gx', even_x)  4.61 us
    ppermute x1, starting transfers between devices, per_device(): odd_side = lax.ppermute(fields, 'gy', odd_y)  4.6 us
    pallas_call x1, Pallas kernels, per_device(): call(contact_kernel, (twelve, twelve, shape(6, 16, 128)), [SMEM_SPEC] + [...  4.13 us
    ppermute x1, waiting for transfers between devices, per_device(): returned = lax.ppermute(back, 'gx', [(i + 1, i) for i in range(31)])  3.26 us
    pallas_call x1, Pallas kernels, per_device(): call(deposit_kernel, (shape(4, 2, 8, 128), shape(3, 64, 128), shape(64, 1...  2.79 us
    all_to_all x1, waiting for transfers between devices, per_device(): every = lax.all_to_all(sums, BOTH, 0, 0, tiled=True)  2.11 us
  transfers between devices with their start and end apart: 9, of which 3 were waited for; matrix products, arithmetic and copies ran while one was open for 0% of the time, Pallas kernels for 15%

profile of v2, /device:TPU:1, one launch (start us, length us, event | category | flops | bytes accessed | tf_op | source)
XLA Modules:
  0.0 54.7 jit_solution(10764379391050827149)
XLA Ops:
  0.6 2.8 %shard_map.103 = (f32[4,2,8,128]{3,2,1,0:T(8,128)S(1)}, f32[3,64,128]{2,1,0:T(8,128)S(1)}, s32[64,128]{1,0:T(8,128)S(1)}, f32[64,128]{1,0:T(8,128)S(1)}, f32[3,8...) custom-call(s32[64,128]{1,0:T(8,128)} %bitcast.13, f32[48,128]{1,0:T(8,128)} %bitcast.15, ...), custom_call_target="tpu_custom_call" | custom-call | tf_op jit(solution)/shard_map/pallas_call | solution.py:551
  3.4 4.6 %collective-permute-start.1 = (f32[4,2,8,128]{3,2,1,0:T(8,128)S(1)}, f32[4,2,8,128]{3,2,1,0:T(8,128)S(1)}, u32[]{:S(2)}, u32[]{:S(2)}) collective-permute-start(f32[4,2,8,128]{3,2,1,0:T(8,128)S(1)} %get-tuple-element.29.own), channel_id=1, source_target_pairs={{1,2},{2,1},{3,4},{4,3},{5,6},{6,5},{9,10},{10,9},{11,12},{12,11},... | collective-permute-start | bytes 98312 | tf_op jit(solution)/shard_map/ppermute | solution.py:576
  8.0 0.1 collective-permute-start
  8.1 0.1 pad_add_fusion.place
  8.2 0.7 %shard_map.104 = (bf16[320,512]{1,0:T(8,128)(2,1)S(1)}, f32[10,16,128]{2,1,0:T(8,128)S(1)}) custom-call(s32[2]{0:T(128)S(1)} %pad_add_fusion.place, f32[3,8192]{1,0:T(4,128)S(1)} %get-tuple-element.23.pos, f32[3,8192]{1,0:T(4,128)S(1)} %get-tuple-element.24.vel, f32[3,8192]{1,0:T(4,128)S(1)} %get-tuple-element.25.spin, ...), custom_call_target="tpu_custom_call" | custom-call | tf_op jit(solution)/shard_map/pallas_call | solution.py:569
  8.9 0.7 %collective-permute-done.1.odd_side = f32[4,2,8,128]{3,2,1,0:T(8,128)S(1)} collective-permute-done((f32[4,2,8,128]{3,2,1,0:T(8,128)S(1)}, f32[4,2,8,128]{3,2,1,0:T(8,128)S(1)}, u32[]{:S(2)}, u32[]{:S(2)}) %collective-permute-start.1) | collective-permute-done | bytes 32800 | tf_op jit(solution)/shard_map/ppermute | solution.py:576
  9.6 0.0 collective-permute-done.even_side
  9.6 0.6 %shard_map.105 = (f32[96,128]{1,0:T(8,128)S(1)}, f32[4,2,8,128]{3,2,1,0:T(8,128)S(1)}) custom-call(s32[2]{0:T(128)S(1)} %pad_add_fusion.place, f32[4,2,8,128]{3,2,1,0:T(8,128)S(1)} %get-tuple-element.29.own, f32[4,2,8,128]{3,2,1,0:T(8,128)S(1)} %collective-permute-done.even_side, f32[4,2,8,128]{3,2,1,0:T(8,128)S(1)} %collective-permute-done.1.odd_side), custom_call_target="tpu_custom_call" | custom-call | tf_op jit(solution)/shard_map/pallas_call | solution.py:577
  10.2 0.7 %collective-permute-start.3 = (f32[96,128]{1,0:T(8,128)S(1)}, f32[96,128]{1,0:T(8,128)S(1)}, u32[]{:S(2)}, u32[]{:S(2)}) collective-permute-start(f32[96,128]{1,0:T(8,128)S(1)} %get-tuple-element.33.own), channel_id=1, source_target_pairs={{8,16},{16,8},{24,32},{32,24},{40,48},{48,40},{56,64},{64,56},{72,... | collective-permute-start | bytes 147464 | tf_op jit(solution)/shard_map/ppermute | solution.py:583
  10.9 4.6 %collective-permute-start.2 = (f32[96,128]{1,0:T(8,128)S(1)}, f32[96,128]{1,0:T(8,128)S(1)}, u32[]{:S(2)}, u32[]{:S(2)}) collective-permute-start(f32[96,128]{1,0:T(8,128)S(1)} %get-tuple-element.33.own), channel_id=1, source_target_pairs={{0,8},{8,0},{16,24},{24,16},{32,40},{40,32},{48,56},{56,48},{64,72... | collective-permute-start | bytes 147464 | tf_op jit(solution)/shard_map/ppermute | solution.py:585
  15.5 0.7 %collective-permute-start.5 = (f32[4,2,8,128]{3,2,1,0:T(8,128)S(1)}, f32[4,2,8,128]{3,2,1,0:T(8,128)S(1)}, u32[]{:S(2)}, u32[]{:S(2)}) collective-permute-start(f32[4,2,8,128]{3,2,1,0:T(8,128)S(1)} %get-tuple-element.34), channel_id=1, source_target_pairs={{16,32},{24,40},{32,16},{40,24},{48,64},{56,72},{64,48},{72,56},{8... | collective-permute-start | bytes 98312 | tf_op jit(solution)/shard_map/ppermute | solution.py:584
  16.1 6.7 %collective-permute-start.4 = (f32[4,2,8,128]{3,2,1,0:T(8,128)S(1)}, f32[4,2,8,128]{3,2,1,0:T(8,128)S(1)}, u32[]{:S(2)}, u32[]{:S(2)}) collective-permute-start(f32[4,2,8,128]{3,2,1,0:T(8,128)S(1)} %get-tuple-element.34), channel_id=1, source_target_pairs={{0,16},{8,24},{16,0},{24,8},{32,48},{40,56},{48,32},{56,40},{64,80... | collective-permute-start | bytes 98312 | tf_op jit(solution)/shard_map/ppermute | solution.py:586
  23.5 1.9 %collective-permute-start.6 = (f32[10,16,128]{2,1,0:T(8,128)S(1)}, f32[10,16,128]{2,1,0:T(8,128)S(1)}, u32[]{:S(2)}, u32[]{:S(2)}) collective-permute-start(f32[10,16,128]{2,1,0:T(8,128)S(1)} %get-tuple-element.37), channel_id=1, source_target_pairs={{0,8},{8,16},{16,24},{24,32},{32,40},{40,48},{48,56},{56,64},{64,7... | collective-permute-start | bytes 245768 | tf_op jit(solution)/shard_map/ppermute | solution.py:587
  25.4 0.0 collective-permute-done.5.far_b
  25.5 0.0 collective-permute-done.4.far_a
  25.5 0.0 collective-permute-done.3.near_b
  25.5 0.0 collective-permute-done.2.near_a
  25.5 1.5 %shard_map.106 = (f32[256,128]{1,0:T(8,128)}, f32[3,2,8,128]{3,2,1,0:T(8,128)S(1)}) custom-call(s32[2]{0:T(128)S(1)} %pad_add_fusion.place, f32[96,128]{1,0:T(8,128)S(1)} %get-tuple-element.33.own, f32[96,128]{1,0:T(8,128)S(1)} %collective-permute-done.2.near_a, f32[96,128]{1,0:T(8,128)S(1)} %collective-permute-done.3.near_b, ...), custom_call_target="tpu_custom_call" | custom-call | flops 8000000000 | tf_op jit(solution)/shard_map/pallas_call | solution.py:588
  27.0 0.0 copy-start
  27.0 14.1 %all-to-all-start = ((f32[256,1,128]{2,1,0:T(1,128)}), f32[256,1,128]{2,1,0:T(1,128)S(1)}, u32[]{:S(2)}, u32[]{:S(2)}) async-start(f32[256,1,128]{2,1,0:T(1,128)} %bitcast.7), calls=%async_computation | async-start | bytes 262144 | tf_op jit(solution)/shard_map/all_to_all | solution.py:591
  41.1 0.0 collective-permute-done.6.ghost
  41.1 0.0 copy-done
  41.2 4.1 %shard_map.107 = (f32[12,32,128]{2,1,0:T(8,128)S(1)}, f32[12,32,128]{2,1,0:T(8,128)S(1)}, f32[6,16,128]{2,1,0:T(8,128)S(1)}) custom-call(s32[1]{0:T(128)S(6)} %copy.12.live, s32[128,128]{1,0:T(8,128)S(1)} %bitcast.11, bf16[320,512]{1,0:T(8,128)(2,1)S(1)} %get-tuple-element.36.table, f32[10,16,128]{2,1,0:T(8,128)S(1)} %collective-permute-done.6.ghost), custom_call_target="tpu_custom_call" | custom-call | flops 2000000000 | tf_op jit(solution)/shard_map/pallas_call | solution.py:597
  45.3 1.3 %collective-permute-start.7 = (f32[6,16,128]{2,1,0:T(8,128)S(1)}, f32[6,16,128]{2,1,0:T(8,128)S(1)}, u32[]{:S(2)}, u32[]{:S(2)}) collective-permute-start(f32[6,16,128]{2,1,0:T(8,128)S(1)} %get-tuple-element.40), channel_id=1, source_target_pairs={{8,0},{16,8},{24,16},{32,24},{40,32},{48,40},{56,48},{64,56},{72,6... | collective-permute-start | bytes 147464 | tf_op jit(solution)/shard_map/ppermute | solution.py:604
  46.6 1.9 %shard_map.108.total = f32[6,64,128]{2,1,0:T(8,128)S(1)} custom-call(s32[1]{0:T(128)S(6)} %copy.12.live, s32[128,128]{1,0:T(8,128)S(1)} %bitcast.12, f32[12,32,128]{2,1,0:T(8,128)S(1)} %get-tuple-element.38.parts_p, f32[12,32,128]{2,1,0:T(8,128)S(1)} %get-tuple-element.39.parts_q), custom_call_target="tpu_custom_call" | custom-call | flops 1000000000 | tf_op jit(solution)/shard_map/pallas_call | solution.py:605
  48.5 3.3 %collective-permute-done.7.returned = f32[6,16,128]{2,1,0:T(8,128)S(1)} collective-permute-done((f32[6,16,128]{2,1,0:T(8,128)S(1)}, f32[6,16,128]{2,1,0:T(8,128)S(1)}, u32[]{:S(2)}, u32[]{:S(2)}) %collective-permute-start.7) | collective-permute-done | bytes 49184 | tf_op jit(solution)/shard_map/ppermute | solution.py:604
  51.8 2.1 %all-to-all-done = f32[256,1,128]{2,1,0:T(1,128)S(1)} async-done(((f32[256,1,128]{2,1,0:T(1,128)}), f32[256,1,128]{2,1,0:T(1,128)S(1)}, u32[]{:S(2)}, u32[]{:S(2)}) %all-to-all-start) | async-done | bytes 131104 | tf_op jit(solution)/shard_map/all_to_all | solution.py:591
  53.9 0.8 %shard_map.109 = (f32[3,8192]{1,0:T(4,128)}, f32[3,8192]{1,0:T(4,128)}, f32[2,8,128]{2,1,0:T(8,128)}) custom-call(f32[6,64,128]{2,1,0:T(8,128)S(1)} %shard_map.108.total, f32[6,16,128]{2,1,0:T(8,128)S(1)} %collective-permute-done.7.returned, f32[3,64,128]{2,1,0:T(8,128)S(1)} %get-tuple-element.41.drag, f32[256,128]{1,0:T(8,128)S(1)} %bitcast.10, ...), custom_call_target="tpu_custom_call" | custom-call | tf_op jit(solution)/shard_map/pallas_call | solution.py:612
Async XLA Ops:
  3.4 6.2 %collective-permute-start.1 = (f32[4,2,8,128]{3,2,1,0:T(8,128)S(1)}, f32[4,2,8,128]{3,2,1,0:T(8,128)S(1)}, u32[]{:S(2)}, u32[]{:S(2)}) collective-permute-start(f32[4,2,8,128]{3,2,1,0:T(8,128)S(1)} %get-tuple-element.29.own), channel_id=1, source_target_pairs={{1,2},{2,1},{3,4},{4,3},{5,6},{6,5},{9,10},{10,9},{11,12},{12,11},... | collective-permute-start | bytes 98312 | tf_op jit(solution)/shard_map/ppermute | solution.py:576
  8.0 1.6 %collective-permute-start = (f32[4,2,8,128]{3,2,1,0:T(8,128)S(1)}, f32[4,2,8,128]{3,2,1,0:T(8,128)S(1)}, u32[]{:S(2)}, u32[]{:S(2)}) collective-permute-start(f32[4,2,8,128]{3,2,1,0:T(8,128)S(1)} %get-tuple-element.29.own), channel_id=1, source_target_pairs={{0,1},{1,0},{2,3},{3,2},{4,5},{5,4},{6,7},{7,6},{8,9},{9,8},{10,11... | collective-permute-start | bytes 98312 | tf_op jit(solution)/shard_map/ppermute | solution.py:575
  10.2 15.3 %collective-permute-start.3 = (f32[96,128]{1,0:T(8,128)S(1)}, f32[96,128]{1,0:T(8,128)S(1)}, u32[]{:S(2)}, u32[]{:S(2)}) collective-permute-start(f32[96,128]{1,0:T(8,128)S(1)} %get-tuple-element.33.own), channel_id=1, source_target_pairs={{8,16},{16,8},{24,32},{32,24},{40,48},{48,40},{56,64},{64,56},{72,... | collective-permute-start | bytes 147464 | tf_op jit(solution)/shard_map/ppermute | solution.py:583
  10.9 14.6 %collective-permute-start.2 = (f32[96,128]{1,0:T(8,128)S(1)}, f32[96,128]{1,0:T(8,128)S(1)}, u32[]{:S(2)}, u32[]{:S(2)}) collective-permute-start(f32[96,128]{1,0:T(8,128)S(1)} %get-tuple-element.33.own), channel_id=1, source_target_pairs={{0,8},{8,0},{16,24},{24,16},{32,40},{40,32},{48,56},{56,48},{64,72... | collective-permute-start | bytes 147464 | tf_op jit(solution)/shard_map/ppermute | solution.py:585
  15.5 10.0 %collective-permute-start.5 = (f32[4,2,8,128]{3,2,1,0:T(8,128)S(1)}, f32[4,2,8,128]{3,2,1,0:T(8,128)S(1)}, u32[]{:S(2)}, u32[]{:S(2)}) collective-permute-start(f32[4,2,8,128]{3,2,1,0:T(8,128)S(1)} %get-tuple-element.34), channel_id=1, source_target_pairs={{16,32},{24,40},{32,16},{40,24},{48,64},{56,72},{64,48},{72,56},{8... | collective-permute-start | bytes 98312 | tf_op jit(solution)/shard_map/ppermute | solution.py:584
  16.1 9.3 %collective-permute-start.4 = (f32[4,2,8,128]{3,2,1,0:T(8,128)S(1)}, f32[4,2,8,128]{3,2,1,0:T(8,128)S(1)}, u32[]{:S(2)}, u32[]{:S(2)}) collective-permute-start(f32[4,2,8,128]{3,2,1,0:T(8,128)S(1)} %get-tuple-element.34), channel_id=1, source_target_pairs={{0,16},{8,24},{16,0},{24,8},{32,48},{40,56},{48,32},{56,40},{64,80... | collective-permute-start | bytes 98312 | tf_op jit(solution)/shard_map/ppermute | solution.py:586
  23.5 17.6 %collective-permute-start.6 = (f32[10,16,128]{2,1,0:T(8,128)S(1)}, f32[10,16,128]{2,1,0:T(8,128)S(1)}, u32[]{:S(2)}, u32[]{:S(2)}) collective-permute-start(f32[10,16,128]{2,1,0:T(8,128)S(1)} %get-tuple-element.37), channel_id=1, source_target_pairs={{0,8},{8,16},{16,24},{24,32},{32,40},{40,48},{48,56},{56,64},{64,7... | collective-permute-start | bytes 245768 | tf_op jit(solution)/shard_map/ppermute | solution.py:587
  27.0 14.1 %copy-start = (s32[64,2,128]{2,1,0:T(2,128)S(1)}, s32[64,2,128]{2,1,0:T(2,128)}, u32[]{:S(2)}) copy-start(s32[64,2,128]{2,1,0:T(2,128)} %param.13) | copy-start | bytes 196612
  27.0 26.9 %all-to-all-start = ((f32[256,1,128]{2,1,0:T(1,128)}), f32[256,1,128]{2,1,0:T(1,128)S(1)}, u32[]{:S(2)}, u32[]{:S(2)}) async-start(f32[256,1,128]{2,1,0:T(1,128)} %bitcast.7), calls=%async_computation | async-start | bytes 262144 | tf_op jit(solution)/shard_map/all_to_all | solution.py:591
  45.3 6.5 %collective-permute-start.7 = (f32[6,16,128]{2,1,0:T(8,128)S(1)}, f32[6,16,128]{2,1,0:T(8,128)S(1)}, u32[]{:S(2)}, u32[]{:S(2)}) collective-permute-start(f32[6,16,128]{2,1,0:T(8,128)S(1)} %get-tuple-element.40), channel_id=1, source_target_pairs={{8,0},{16,8},{24,16},{32,24},{40,32},{48,40},{56,48},{64,56},{72,6... | collective-permute-start | bytes 147464 | tf_op jit(solution)/shard_map/ppermute | solution.py:604

commit v3 on v2

--- a/solution.py
+++ b/solution.py
@@ -109,7 +109,7 @@
         (cell, fluid, radius, vel, pos, spin),
         sems,
     )
-    for copy in copies[:4]:
+    for copy in copies[:2]:
         copy.wait()
     fluid_high, fluid_low = split(fluid[...])
     fluid_table = jnp.concatenate([fluid_high, fluid_low], axis=1)
@@ -122,6 +122,9 @@
         seen = jnp.dot(
             fluid_table, jnp.concatenate([hot, hot], axis=0), preferred_element_type=F32
         )
+        if g == 0:
+            for copy in copies[2:4]:
+                copy.wait()
         rad = radius[rows, :]
         values = []
         for d in range(3):
@@ -158,7 +161,8 @@
         copy.wait()
 
 
-def table_kernel(place, pos, vel, spin, radius, cell, table, border):
+def table_kernel(pos, vel, spin, radius, cell, table, border):
+    place = (lax.axis_index("gx"), lax.axis_index("gy"))
     cells = cell[...]
     rad = radius[...]
     corner = [
@@ -255,7 +259,10 @@
     return force, twist
 
 
-def contact_kernel(live, pairs, table, ghost, parts_p, parts_q, back, first, second, full, sum_far):
+def contact_kernel(
+    live, pairs, table, ghost,
+    parts_p, parts_q, back, total, first, second, full, sum_far, sum_p, sum_q,
+):
     count = live[0]
     full[0:320, :] = table[...]
     pieces = [
@@ -308,8 +315,17 @@
         back[f, 0:8, :] = rows[:, 0:128]
         back[f, 8:16, :] = rows[:, 128:256]
 
-
-def own_kernel(live, pairs, parts_p, parts_q, total, sum_p, sum_q):
+    @pl.when(early())
+    def _():
+        own_sums(live, pairs, parts_p, parts_q, total, sum_p, sum_q)
+
+
+def early():
+    gx = lax.axis_index("gx")
+    return (gx > 0) & ((gx & 7) == 0)
+
+
+def own_sums(live, pairs, parts_p, parts_q, total, sum_p, sum_q):
     sum_p[...] = jnp.zeros_like(sum_p)
     sum_q[...] = jnp.zeros_like(sum_q)
 
@@ -341,6 +357,16 @@
         total[f, 32:64, :] = own[:, 128:256]
 
 
+def own_kernel(live, pairs, parts_p, parts_q, before, total, sum_p, sum_q):
+    @pl.when(early())
+    def _():
+        total[...] = before[...]
+
+    @pl.when(jnp.logical_not(early()))
+    def _():
+        own_sums(live, pairs, parts_p, parts_q, total, sum_p, sum_q)
+
+
 def finish_kernel(total, returned, drag, sums, basis, force_out, twist_out, pressure):
     solve(sums, basis, pressure)
     for f in range(3):
@@ -365,8 +391,8 @@
     return pltpu.roll(x, 1, 0)
 
 
-def rows_kernel(place, own, even_side, odd_side, near, slim):
-    even = (place[1] & 1) == 0
+def rows_kernel(own, even_side, odd_side, near, slim):
+    even = (lax.axis_index("gy") & 1) == 0
     sub = lax.broadcasted_iota(jnp.int32, (8, 128), 0)
 
     def extend(f, layer):
@@ -394,8 +420,8 @@
 SHIFT = 3.0
 
 
-def krylov_kernel(place, own, near_a, near_b, far_a, far_b, sums, basis):
-    gx, gy = place[0], place[1]
+def krylov_kernel(own, near_b, near_a, far_b, far_a, sums, basis):
+    gx, gy = lax.axis_index("gx"), lax.axis_index("gy")
     up_a = (gx & 1) == 0
     far_up_a = (gx & 2) == 0
     blank = jnp.zeros((8, 128), F32)
@@ -538,7 +564,6 @@
 
 
 def per_device(pos, vel, spin, radius, cell, pairs, live, fluid):
-    place = jnp.stack([lax.axis_index("gx"), lax.axis_index("gy")]).astype(jnp.int32)
     radius = radius.reshape(64, 128)
     cell = cell.reshape(64, 128)
     pairs = pairs.reshape(128, 128)
@@ -569,16 +594,16 @@
     table, border = call(
         table_kernel,
         (shape(320, 512, dtype=BF16), shape(10, 16, 128)),
-        [SMEM_SPEC] + [VMEM_SPEC] * 5,
-    )(place, pos, vel, spin, radius, cell)
+        [VMEM_SPEC] * 5,
+    )(pos, vel, spin, radius, cell)
 
     even_side = lax.ppermute(fields, "gy", even_y)
     odd_side = lax.ppermute(fields, "gy", odd_y)
     near, slim = call(
         rows_kernel,
         (shape(96, 128), shape(4, 2, 8, 128)),
-        [SMEM_SPEC] + [VMEM_SPEC] * 3,
-    )(place, fields, even_side, odd_side)
+        [VMEM_SPEC] * 3,
+    )(fields, even_side, odd_side)
     near, slim, border = lax.optimization_barrier((near, slim, border))
     near_b = lax.ppermute(near, "gx", odd_x)
     far_b = lax.ppermute(slim, "gx", [(i, ((i + 2) ^ 2) - 2) for i in range(2, 30)])
@@ -586,29 +611,36 @@
     far_a = lax.ppermute(slim, "gx", [(i, i ^ 2) for i in range(32)])
     ghost = lax.ppermute(border, "gx", [(i, i + 1) for i in range(31)])
     sums, basis = call(
-        krylov_kernel, (shape(256, 128), shape(3, 2, 8, 128)), [SMEM_SPEC] + [VMEM_SPEC] * 5, cost=work(8),
-    )(place, near, near_a, near_b, far_a, far_b)
+        krylov_kernel, (shape(256, 128), shape(3, 2, 8, 128)), [VMEM_SPEC] * 5, cost=work(8),
+    )(near, near_b, near_a, far_b, far_a)
     every = lax.all_to_all(sums, BOTH, 0, 0, tiled=True)
 
     table, sums = lax.optimization_barrier((table, sums))
     sums_384 = pltpu.VMEM((384, 256), F32)
     found = pltpu.VMEM((10, BLOCKS, 128), F32)
     twelve = shape(12, BLOCKS, 128)
-    parts_p, parts_q, back = call(
+    parts_p, parts_q, back, before = call(
         contact_kernel,
-        (twelve, twelve, shape(6, 16, 128)),
+        (twelve, twelve, shape(6, 16, 128), shape(6, 64, 128)),
         [SMEM_SPEC] + [VMEM_SPEC] * 3,
-        scratch=[found, found, pltpu.VMEM((400, 512), BF16), pltpu.VMEM((192, 256), F32)],
+        scratch=[
+            found,
+            found,
+            pltpu.VMEM((400, 512), BF16),
+            pltpu.VMEM((192, 256), F32),
+            sums_384,
+            sums_384,
+        ],
         cost=work(2),
     )(live, pairs, table, ghost)
     returned = lax.ppermute(back, "gx", [(i + 1, i) for i in range(31)])
     total = call(
         own_kernel,
         shape(6, 64, 128),
-        [SMEM_SPEC] + [VMEM_SPEC] * 3,
+        [SMEM_SPEC] + [VMEM_SPEC] * 4,
         scratch=[sums_384, sums_384],
         cost=work(1),
-    )(live, pairs, parts_p, parts_q)
+    )(live, pairs, parts_p, parts_q, before)
     return call(
         finish_kernel,
         (shape(3, 8192), shape(3, 8192), shape(2, 8, 128)),

time: 55.5 us -> 52.9 us (0.953)
  waiting for transfers between devices: 6.1 us -> 4.75 us
  starting transfers between devices: 34.7 us -> 33.5 us
    ppermute x1, starting transfers between devices: 1.93 us -> 5.48 us  [per_device(): ghost = lax.ppermute(border, 'gx', [(i, i + 1) for i in range(31)])]
    ppermute x1, starting transfers between devices: 4.61 us -> 1.74 us  [per_device(): near_a = lax.ppermute(near, 'gx', even_x)]
    ppermute x1, starting transfers between devices: 6.73 us -> 4.32 us  [per_device(): far_a = lax.ppermute(slim, 'gx', [(i, i ^ 2) for i in range(32)])]
    ppermute x1, waiting for transfers between devices: 3.26 us -> 1.26 us  [per_device(): returned = lax.ppermute(back, 'gx', [(i + 1, i) for i in range(31)])]
    ppermute x1, waiting for transfers between devices: 0.71 us -> 1.32 us  [per_device(): odd_side = lax.ppermute(fields, 'gy', odd_y)]
  transfers between devices with their start and end apart: 9 -> 9, of which waited for: 3 -> 3; matrix products, arithmetic and copies ran while one was open for 0% -> 0% of each run, Pallas kernels for 15% -> 18%
where the time goes in v3:
time: 52.9 us; the launch traced here: 52.4 us
  starting transfers between devices  33.5 us (63%)
  Pallas kernels  12.7 us (24%)
  waiting for transfers between devices  4.75 us (9%)
  between operations  1.42 us (3%)
    all_to_all x1, starting transfers between devices, per_device(): every = lax.all_to_all(sums, BOTH, 0, 0, tiled=True)  14.6 us
    ppermute x1, starting transfers between devices, per_device(): ghost = lax.ppermute(border, 'gx', [(i, i + 1) for i in range(31)])  5.48 us
    pallas_call x1, Pallas kernels, per_device(): call(contact_kernel, (twelve, twelve, shape(6, 16, 128), shape(6, 64, 128...  5.47 us
    ppermute x1, starting transfers between devices, per_device(): odd_side = lax.ppermute(fields, 'gy', odd_y)  4.58 us
    ppermute x1, starting transfers between devices, per_device(): far_a = lax.ppermute(slim, 'gx', [(i, i ^ 2) for i in range(32)])  4.32 us
    pallas_call x1, Pallas kernels, per_device(): call(deposit_kernel, (shape(4, 2, 8, 128), shape(3, 64, 128), shape(64, 1...  2.73 us
    pallas_call x1, Pallas kernels, per_device(): call(own_kernel, shape(6, 64, 128), [SMEM_SPEC] + [VMEM_SPEC] * 4, scratc...  2.56 us
    all_to_all x1, waiting for transfers between devices, per_device(): every = lax.all_to_all(sums, BOTH, 0, 0, tiled=True)  2.15 us
  transfers between devices with their start and end apart: 9, of which 3 were waited for; matrix products, arithmetic and copies ran while one was open for 0% of the time, Pallas kernels for 18%

profile of v3, /device:TPU:1, one launch (start us, length us, event | category | flops | bytes accessed | tf_op | source)
XLA Modules:
  0.0 52.4 jit_solution(9171489151429602094)
XLA Ops:
  0.6 2.7 %shard_map.103 = (f32[4,2,8,128]{3,2,1,0:T(8,128)S(1)}, f32[3,64,128]{2,1,0:T(8,128)S(1)}, s32[64,128]{1,0:T(8,128)S(1)}, f32[64,128]{1,0:T(8,128)S(1)}, f32[3,8...) custom-call(s32[64,128]{1,0:T(8,128)} %bitcast.11, f32[48,128]{1,0:T(8,128)} %bitcast.13, ...), custom_call_target="tpu_custom_call" | custom-call | tf_op jit(solution)/shard_map/pallas_call | solution.py:576
  3.4 4.6 %collective-permute-start.1 = (f32[4,2,8,128]{3,2,1,0:T(8,128)S(1)}, f32[4,2,8,128]{3,2,1,0:T(8,128)S(1)}, u32[]{:S(2)}, u32[]{:S(2)}) collective-permute-start(f32[4,2,8,128]{3,2,1,0:T(8,128)S(1)} %get-tuple-element.30.own), channel_id=1, source_target_pairs={{1,2},{2,1},{3,4},{4,3},{5,6},{6,5},{9,10},{10,9},{11,12},{12,11},... | collective-permute-start | bytes 98312 | tf_op jit(solution)/shard_map/ppermute | solution.py:601
  8.0 0.1 collective-permute-start
  8.1 0.2 shard_map.104
  8.2 1.3 %collective-permute-done.1.odd_side = f32[4,2,8,128]{3,2,1,0:T(8,128)S(1)} collective-permute-done((f32[4,2,8,128]{3,2,1,0:T(8,128)S(1)}, f32[4,2,8,128]{3,2,1,0:T(8,128)S(1)}, u32[]{:S(2)}, u32[]{:S(2)}) %collective-permute-start.1) | collective-permute-done | bytes 32800 | tf_op jit(solution)/shard_map/ppermute | solution.py:601
  9.5 0.0 collective-permute-done.even_side
  9.6 1.7 %collective-permute-start.3 = (f32[96,128]{1,0:T(8,128)S(1)}, f32[96,128]{1,0:T(8,128)S(1)}, u32[]{:S(2)}, u32[]{:S(2)}) collective-permute-start(f32[96,128]{1,0:T(8,128)S(1)} %get-tuple-element.34.own), channel_id=1, source_target_pairs={{0,8},{8,0},{16,24},{24,16},{32,40},{40,32},{48,56},{56,48},{64,72... | collective-permute-start | bytes 147464 | tf_op jit(solution)/shard_map/ppermute | solution.py:610
  11.3 0.7 %collective-permute-start.2 = (f32[96,128]{1,0:T(8,128)S(1)}, f32[96,128]{1,0:T(8,128)S(1)}, u32[]{:S(2)}, u32[]{:S(2)}) collective-permute-start(f32[96,128]{1,0:T(8,128)S(1)} %get-tuple-element.34.own), channel_id=1, source_target_pairs={{8,16},{16,8},{24,32},{32,24},{40,48},{48,40},{56,64},{64,56},{72,... | collective-permute-start | bytes 147464 | tf_op jit(solution)/shard_map/ppermute | solution.py:608
  12.0 4.3 %collective-permute-start.5 = (f32[4,2,8,128]{3,2,1,0:T(8,128)S(1)}, f32[4,2,8,128]{3,2,1,0:T(8,128)S(1)}, u32[]{:S(2)}, u32[]{:S(2)}) collective-permute-start(f32[4,2,8,128]{3,2,1,0:T(8,128)S(1)} %get-tuple-element.35), channel_id=1, source_target_pairs={{0,16},{8,24},{16,0},{24,8},{32,48},{40,56},{48,32},{56,40},{64,80... | collective-permute-start | bytes 98312 | tf_op jit(solution)/shard_map/ppermute | solution.py:611
  16.3 0.7 %collective-permute-start.4 = (f32[4,2,8,128]{3,2,1,0:T(8,128)S(1)}, f32[4,2,8,128]{3,2,1,0:T(8,128)S(1)}, u32[]{:S(2)}, u32[]{:S(2)}) collective-permute-start(f32[4,2,8,128]{3,2,1,0:T(8,128)S(1)} %get-tuple-element.35), channel_id=1, source_target_pairs={{16,32},{24,40},{32,16},{40,24},{48,64},{56,72},{64,48},{72,56},{8... | collective-permute-start | bytes 98312 | tf_op jit(solution)/shard_map/ppermute | solution.py:609
  17.6 5.5 %collective-permute-start.6 = (f32[10,16,128]{2,1,0:T(8,128)S(1)}, f32[10,16,128]{2,1,0:T(8,128)S(1)}, u32[]{:S(2)}, u32[]{:S(2)}) collective-permute-start(f32[10,16,128]{2,1,0:T(8,128)S(1)} %get-tuple-element.38), channel_id=1, source_target_pairs={{0,8},{8,16},{16,24},{24,32},{32,40},{40,48},{48,56},{56,64},{64,7... | collective-permute-start | bytes 245768 | tf_op jit(solution)/shard_map/ppermute | solution.py:612
  23.1 0.0 collective-permute-done.5.far_a
  23.1 0.0 collective-permute-done.4.far_b
  23.1 0.0 collective-permute-done.3.near_a
  23.1 0.0 collective-permute-done.2.near_b
  23.1 1.0 %shard_map.106 = (f32[256,128]{1,0:T(8,128)}, f32[3,2,8,128]{3,2,1,0:T(8,128)S(1)}) custom-call(f32[96,128]{1,0:T(8,128)S(1)} %get-tuple-element.34.own, f32[96,128]{1,0:T(8,128)S(1)} %collective-permute-done.2.near_b, f32[96,128]{1,0:T(8,128)S(1)} %collective-permute-done.3.near_a, f32[4,2,8,128]{3,2,1,0:T(8,128)S(1)} %collective-permute-done.4.far_b, ...), custom_call_target="tpu_custom_call" | custom-call | flops 8000000000 | tf_op jit(solution)/shard_map/pallas_call | solution.py:613
  24.1 0.0 copy-start
  24.1 14.6 %all-to-all-start = ((f32[256,1,128]{2,1,0:T(1,128)}), f32[256,1,128]{2,1,0:T(1,128)S(1)}, u32[]{:S(2)}, u32[]{:S(2)}) async-start(f32[256,1,128]{2,1,0:T(1,128)} %bitcast.5), calls=%async_computation | async-start | bytes 262144 | tf_op jit(solution)/shard_map/all_to_all | solution.py:616
  38.8 0.0 collective-permute-done.6.ghost
  38.8 0.0 copy-done
  38.8 5.5 %shard_map.107 = (f32[12,32,128]{2,1,0:T(8,128)S(1)}, f32[12,32,128]{2,1,0:T(8,128)S(1)}, f32[6,16,128]{2,1,0:T(8,128)S(1)}, f32[6,64,128]{2,1,0:T(8,128)S(1)}) custom-call(s32[1]{0:T(128)S(6)} %copy.12.live, s32[128,128]{1,0:T(8,128)S(1)} %bitcast.9, bf16[320,512]{1,0:T(8,128)(2,1)S(1)} %get-tuple-element.37.table, ...), custom_call_target="tpu_custom_call" | custom-call | flops 2000000000 | tf_op jit(solution)/shard_map/pallas_call | solution.py:622
  44.3 1.3 %collective-permute-start.7 = (f32[6,16,128]{2,1,0:T(8,128)S(1)}, f32[6,16,128]{2,1,0:T(8,128)S(1)}, u32[]{:S(2)}, u32[]{:S(2)}) collective-permute-start(f32[6,16,128]{2,1,0:T(8,128)S(1)} %get-tuple-element.42), channel_id=1, source_target_pairs={{8,0},{16,8},{24,16},{32,24},{40,32},{48,40},{56,48},{64,56},{72,6... | collective-permute-start | bytes 147464 | tf_op jit(solution)/shard_map/ppermute | solution.py:636
  45.6 2.6 %shard_map.108.total = f32[6,64,128]{2,1,0:T(8,128)S(1)} custom-call(s32[1]{0:T(128)S(6)} %copy.12.live, s32[128,128]{1,0:T(8,128)S(1)} %bitcast.10, f32[12,32,128]{2,1,0:T(8,128)S(1)} %get-tuple-element.39.parts_p, f32[12,32,128]{2,1,0:T(8,128)S(1)} %get-tuple-element.40.parts_q, f32[6,64,128]{2,1,0:T(8,128)S(1)} %get-tuple-element.41.before), custom_call_target="tpu_custom_call" | custom-call | flops 1000000000 | tf_op jit(solution)/shard_map/pallas_call | solution.py:637
  48.2 1.3 %collective-permute-done.7.returned = f32[6,16,128]{2,1,0:T(8,128)S(1)} collective-permute-done((f32[6,16,128]{2,1,0:T(8,128)S(1)}, f32[6,16,128]{2,1,0:T(8,128)S(1)}, u32[]{:S(2)}, u32[]{:S(2)}) %collective-permute-start.7) | collective-permute-done | bytes 49184 | tf_op jit(solution)/shard_map/ppermute | solution.py:636
  49.4 2.2 %all-to-all-done = f32[256,1,128]{2,1,0:T(1,128)S(1)} async-done(((f32[256,1,128]{2,1,0:T(1,128)}), f32[256,1,128]{2,1,0:T(1,128)S(1)}, u32[]{:S(2)}, u32[]{:S(2)}) %all-to-all-start) | async-done | bytes 131104 | tf_op jit(solution)/shard_map/all_to_all | solution.py:616
  51.6 0.8 %shard_map.109 = (f32[3,8192]{1,0:T(4,128)}, f32[3,8192]{1,0:T(4,128)}, f32[2,8,128]{2,1,0:T(8,128)}) custom-call(f32[6,64,128]{2,1,0:T(8,128)S(1)} %shard_map.108.total, f32[6,16,128]{2,1,0:T(8,128)S(1)} %collective-permute-done.7.returned, f32[3,64,128]{2,1,0:T(8,128)S(1)} %get-tuple-element.43.drag, f32[256,128]{1,0:T(8,128)S(1)} %bitcast.8, ...), custom_call_target="tpu_custom_call" | custom-call | tf_op jit(solution)/shard_map/pallas_call | solution.py:644
  (1 shorter events, 0.0 us)
Async XLA Ops:
  3.4 6.2 %collective-permute-start.1 = (f32[4,2,8,128]{3,2,1,0:T(8,128)S(1)}, f32[4,2,8,128]{3,2,1,0:T(8,128)S(1)}, u32[]{:S(2)}, u32[]{:S(2)}) collective-permute-start(f32[4,2,8,128]{3,2,1,0:T(8,128)S(1)} %get-tuple-element.30.own), channel_id=1, source_target_pairs={{1,2},{2,1},{3,4},{4,3},{5,6},{6,5},{9,10},{10,9},{11,12},{12,11},... | collective-permute-start | bytes 98312 | tf_op jit(solution)/shard_map/ppermute | solution.py:601
  8.0 1.6 %collective-permute-start = (f32[4,2,8,128]{3,2,1,0:T(8,128)S(1)}, f32[4,2,8,128]{3,2,1,0:T(8,128)S(1)}, u32[]{:S(2)}, u32[]{:S(2)}) collective-permute-start(f32[4,2,8,128]{3,2,1,0:T(8,128)S(1)} %get-tuple-element.30.own), channel_id=1, source_target_pairs={{0,1},{1,0},{2,3},{3,2},{4,5},{5,4},{6,7},{7,6},{8,9},{9,8},{10,11... | collective-permute-start | bytes 98312 | tf_op jit(solution)/shard_map/ppermute | solution.py:600
  9.6 13.5 %collective-permute-start.3 = (f32[96,128]{1,0:T(8,128)S(1)}, f32[96,128]{1,0:T(8,128)S(1)}, u32[]{:S(2)}, u32[]{:S(2)}) collective-permute-start(f32[96,128]{1,0:T(8,128)S(1)} %get-tuple-element.34.own), channel_id=1, source_target_pairs={{0,8},{8,0},{16,24},{24,16},{32,40},{40,32},{48,56},{56,48},{64,72... | collective-permute-start | bytes 147464 | tf_op jit(solution)/shard_map/ppermute | solution.py:610
  11.3 11.8 %collective-permute-start.2 = (f32[96,128]{1,0:T(8,128)S(1)}, f32[96,128]{1,0:T(8,128)S(1)}, u32[]{:S(2)}, u32[]{:S(2)}) collective-permute-start(f32[96,128]{1,0:T(8,128)S(1)} %get-tuple-element.34.own), channel_id=1, source_target_pairs={{8,16},{16,8},{24,32},{32,24},{40,48},{48,40},{56,64},{64,56},{72,... | collective-permute-start | bytes 147464 | tf_op jit(solution)/shard_map/ppermute | solution.py:608
  12.0 11.1 %collective-permute-start.5 = (f32[4,2,8,128]{3,2,1,0:T(8,128)S(1)}, f32[4,2,8,128]{3,2,1,0:T(8,128)S(1)}, u32[]{:S(2)}, u32[]{:S(2)}) collective-permute-start(f32[4,2,8,128]{3,2,1,0:T(8,128)S(1)} %get-tuple-element.35), channel_id=1, source_target_pairs={{0,16},{8,24},{16,0},{24,8},{32,48},{40,56},{48,32},{56,40},{64,80... | collective-permute-start | bytes 98312 | tf_op jit(solution)/shard_map/ppermute | solution.py:611
  16.3 6.8 %collective-permute-start.4 = (f32[4,2,8,128]{3,2,1,0:T(8,128)S(1)}, f32[4,2,8,128]{3,2,1,0:T(8,128)S(1)}, u32[]{:S(2)}, u32[]{:S(2)}) collective-permute-start(f32[4,2,8,128]{3,2,1,0:T(8,128)S(1)} %get-tuple-element.35), channel_id=1, source_target_pairs={{16,32},{24,40},{32,16},{40,24},{48,64},{56,72},{64,48},{72,56},{8... | collective-permute-start | bytes 98312 | tf_op jit(solution)/shard_map/ppermute | solution.py:609
  17.6 21.2 %collective-permute-start.6 = (f32[10,16,128]{2,1,0:T(8,128)S(1)}, f32[10,16,128]{2,1,0:T(8,128)S(1)}, u32[]{:S(2)}, u32[]{:S(2)}) collective-permute-start(f32[10,16,128]{2,1,0:T(8,128)S(1)} %get-tuple-element.38), channel_id=1, source_target_pairs={{0,8},{8,16},{16,24},{24,32},{32,40},{40,48},{48,56},{56,64},{64,7... | collective-permute-start | bytes 245768 | tf_op jit(solution)/shard_map/ppermute | solution.py:612
  24.1 14.7 %copy-start = (s32[64,2,128]{2,1,0:T(2,128)S(1)}, s32[64,2,128]{2,1,0:T(2,128)}, u32[]{:S(2)}) copy-start(s32[64,2,128]{2,1,0:T(2,128)} %param.13) | copy-start | bytes 196612
  24.1 27.4 %all-to-all-start = ((f32[256,1,128]{2,1,0:T(1,128)}), f32[256,1,128]{2,1,0:T(1,128)S(1)}, u32[]{:S(2)}, u32[]{:S(2)}) async-start(f32[256,1,128]{2,1,0:T(1,128)} %bitcast.5), calls=%async_computation | async-start | bytes 262144 | tf_op jit(solution)/shard_map/all_to_all | solution.py:616
  44.3 5.1 %collective-permute-start.7 = (f32[6,16,128]{2,1,0:T(8,128)S(1)}, f32[6,16,128]{2,1,0:T(8,128)S(1)}, u32[]{:S(2)}, u32[]{:S(2)}) collective-permute-start(f32[6,16,128]{2,1,0:T(8,128)S(1)} %get-tuple-element.42), channel_id=1, source_target_pairs={{8,0},{16,8},{24,16},{32,24},{40,32},{48,40},{56,48},{64,56},{72,6... | collective-permute-start | bytes 147464 | tf_op jit(solution)/shard_map/ppermute | solution.py:636

commit v4 on v3

--- a/solution.py
+++ b/solution.py
@@ -142,7 +142,7 @@
             high, low = halves(value)
             parts[k, rows, :] = high
             parts[4 + k, rows, :] = low
-        masks = tiles(as_bf16(mask))
+        masks = tiles(hot_rows(16, cells >> 7))
         left = [
             jnp.concatenate([spread(parts, v, 8 * g + k, masks[k : k + 1])[0] for v in range(8)], 0)
             for k in range(8)
@@ -299,7 +299,7 @@
     def step(it, carry):
         row, place = second_index(pair_block(pairs, it))
         hot = hot_rows(256, place)
-        far = as_bf16(one_hot(16, row - 32))
+        far = hot_rows(16, row - 32)
         left = [
             jnp.concatenate(
                 sum([spread(parts_q, v, it * 8 + k, [m]) for v in range(12)], []), axis=0
@@ -337,7 +337,7 @@
         ):
             row, place = index(block)
             hot = hot_rows(256, place)
-            mask = as_bf16(one_hot(32, row))
+            mask = hot_rows(32, row)
             left = [
                 jnp.concatenate(
                     sum([spread(parts, v, it * 8 + k, [m[0:16], m[16:32]]) for v in range(12)], []),

time: 52.9 us -> 52.8 us (level)
  waiting for transfers between devices: 4.75 us -> 10.6 us
  Pallas kernels: 12.7 us -> 6.89 us
    pallas_call x1, Pallas kernels: 5.47 us -> 1.48 us  [per_device(): call(contact_kernel, (twelve, twelve, shape(6, 16, 128), shape(6, 64, 128...]
    ppermute x1, waiting for transfers between devices: 1.26 us -> 4.48 us  [per_device(): returned = lax.ppermute(back, 'gx', [(i + 1, i) for i in range(31)])]
    all_to_all x1, waiting for transfers between devices: 2.15 us -> 4.76 us  [per_device(): every = lax.all_to_all(sums, BOTH, 0, 0, tiled=True)]
    pallas_call x1, Pallas kernels: 2.56 us -> 0.72 us  [per_device(): call(own_kernel, shape(6, 64, 128), [SMEM_SPEC] + [VMEM_SPEC] * 4, scratc...]
  transfers between devices with their start and end apart: 9 -> 9, of which waited for: 3 -> 3; matrix products, arithmetic and copies ran while one was open for 0% -> 0% of each run, Pallas kernels for 18% -> 6%
where the time goes in v4:
time: 52.8 us; the launch traced here: 52.4 us
  starting transfers between devices  33.5 us (63%)
  waiting for transfers between devices  10.6 us (20%)
  Pallas kernels  6.89 us (13%)
  between operations  1.42 us (3%)
    all_to_all x1, starting transfers between devices, per_device(): every = lax.all_to_all(sums, BOTH, 0, 0, tiled=True)  14.7 us
    ppermute x1, starting transfers between devices, per_device(): ghost = lax.ppermute(border, 'gx', [(i, i + 1) for i in range(31)])  5.47 us
    all_to_all x1, waiting for transfers between devices, per_device(): every = lax.all_to_all(sums, BOTH, 0, 0, tiled=True)  4.76 us
    ppermute x1, starting transfers between devices, per_device(): odd_side = lax.ppermute(fields, 'gy', odd_y)  4.59 us
    ppermute x1, waiting for transfers between devices, per_device(): returned = lax.ppermute(back, 'gx', [(i + 1, i) for i in range(31)])  4.48 us
    ppermute x1, starting transfers between devices, per_device(): far_a = lax.ppermute(slim, 'gx', [(i, i ^ 2) for i in range(32)])  4.34 us
    pallas_call x1, Pallas kernels, per_device(): call(deposit_kernel, (shape(4, 2, 8, 128), shape(3, 64, 128), shape(64, 1...  2.73 us
    ppermute x1, starting transfers between devices, per_device(): near_a = lax.ppermute(near, 'gx', even_x)  1.72 us
  transfers between devices with their start and end apart: 9, of which 3 were waited for; matrix products, arithmetic and copies ran while one was open for 0% of the time, Pallas kernels for 6%

profile of v4, /device:TPU:1, one launch (start us, length us, event | category | flops | bytes accessed | tf_op | source)
XLA Modules:
  0.0 52.4 jit_solution(3446726986906937264)
XLA Ops:
  0.6 2.7 %shard_map.103 = (f32[4,2,8,128]{3,2,1,0:T(8,128)S(1)}, f32[3,64,128]{2,1,0:T(8,128)S(1)}, s32[64,128]{1,0:T(8,128)S(1)}, f32[64,128]{1,0:T(8,128)S(1)}, f32[3,8...) custom-call(s32[64,128]{1,0:T(8,128)} %bitcast.11, f32[48,128]{1,0:T(8,128)} %bitcast.13, ...), custom_call_target="tpu_custom_call" | custom-call | tf_op jit(solution)/shard_map/pallas_call | solution.py:576
  3.4 4.6 %collective-permute-start.1 = (f32[4,2,8,128]{3,2,1,0:T(8,128)S(1)}, f32[4,2,8,128]{3,2,1,0:T(8,128)S(1)}, u32[]{:S(2)}, u32[]{:S(2)}) collective-permute-start(f32[4,2,8,128]{3,2,1,0:T(8,128)S(1)} %get-tuple-element.30.own), channel_id=1, source_target_pairs={{1,2},{2,1},{3,4},{4,3},{5,6},{6,5},{9,10},{10,9},{11,12},{12,11},... | collective-permute-start | bytes 98312 | tf_op jit(solution)/shard_map/ppermute | solution.py:601
  8.0 0.1 collective-permute-start
  8.1 0.2 shard_map.104
  8.2 1.3 %collective-permute-done.1.odd_side = f32[4,2,8,128]{3,2,1,0:T(8,128)S(1)} collective-permute-done((f32[4,2,8,128]{3,2,1,0:T(8,128)S(1)}, f32[4,2,8,128]{3,2,1,0:T(8,128)S(1)}, u32[]{:S(2)}, u32[]{:S(2)}) %collective-permute-start.1) | collective-permute-done | bytes 32800 | tf_op jit(solution)/shard_map/ppermute | solution.py:601
  9.5 0.0 collective-permute-done.even_side
  9.6 1.7 %collective-permute-start.3 = (f32[96,128]{1,0:T(8,128)S(1)}, f32[96,128]{1,0:T(8,128)S(1)}, u32[]{:S(2)}, u32[]{:S(2)}) collective-permute-start(f32[96,128]{1,0:T(8,128)S(1)} %get-tuple-element.34.own), channel_id=1, source_target_pairs={{0,8},{8,0},{16,24},{24,16},{32,40},{40,32},{48,56},{56,48},{64,72... | collective-permute-start | bytes 147464 | tf_op jit(solution)/shard_map/ppermute | solution.py:610
  11.3 0.7 %collective-permute-start.2 = (f32[96,128]{1,0:T(8,128)S(1)}, f32[96,128]{1,0:T(8,128)S(1)}, u32[]{:S(2)}, u32[]{:S(2)}) collective-permute-start(f32[96,128]{1,0:T(8,128)S(1)} %get-tuple-element.34.own), channel_id=1, source_target_pairs={{8,16},{16,8},{24,32},{32,24},{40,48},{48,40},{56,64},{64,56},{72,... | collective-permute-start | bytes 147464 | tf_op jit(solution)/shard_map/ppermute | solution.py:608
  12.0 4.3 %collective-permute-start.5 = (f32[4,2,8,128]{3,2,1,0:T(8,128)S(1)}, f32[4,2,8,128]{3,2,1,0:T(8,128)S(1)}, u32[]{:S(2)}, u32[]{:S(2)}) collective-permute-start(f32[4,2,8,128]{3,2,1,0:T(8,128)S(1)} %get-tuple-element.35), channel_id=1, source_target_pairs={{0,16},{8,24},{16,0},{24,8},{32,48},{40,56},{48,32},{56,40},{64,80... | collective-permute-start | bytes 98312 | tf_op jit(solution)/shard_map/ppermute | solution.py:611
  16.3 0.7 %collective-permute-start.4 = (f32[4,2,8,128]{3,2,1,0:T(8,128)S(1)}, f32[4,2,8,128]{3,2,1,0:T(8,128)S(1)}, u32[]{:S(2)}, u32[]{:S(2)}) collective-permute-start(f32[4,2,8,128]{3,2,1,0:T(8,128)S(1)} %get-tuple-element.35), channel_id=1, source_target_pairs={{16,32},{24,40},{32,16},{40,24},{48,64},{56,72},{64,48},{72,56},{8... | collective-permute-start | bytes 98312 | tf_op jit(solution)/shard_map/ppermute | solution.py:609
  17.6 5.5 %collective-permute-start.6 = (f32[10,16,128]{2,1,0:T(8,128)S(1)}, f32[10,16,128]{2,1,0:T(8,128)S(1)}, u32[]{:S(2)}, u32[]{:S(2)}) collective-permute-start(f32[10,16,128]{2,1,0:T(8,128)S(1)} %get-tuple-element.38), channel_id=1, source_target_pairs={{0,8},{8,16},{16,24},{24,32},{32,40},{40,48},{48,56},{56,64},{64,7... | collective-permute-start | bytes 245768 | tf_op jit(solution)/shard_map/ppermute | solution.py:612
  23.1 0.0 collective-permute-done.5.far_a
  23.1 0.0 collective-permute-done.4.far_b
  23.1 0.0 collective-permute-done.3.near_a
  23.1 0.0 collective-permute-done.2.near_b
  23.1 1.0 %shard_map.106 = (f32[256,128]{1,0:T(8,128)}, f32[3,2,8,128]{3,2,1,0:T(8,128)S(1)}) custom-call(f32[96,128]{1,0:T(8,128)S(1)} %get-tuple-element.34.own, f32[96,128]{1,0:T(8,128)S(1)} %collective-permute-done.2.near_b, f32[96,128]{1,0:T(8,128)S(1)} %collective-permute-done.3.near_a, f32[4,2,8,128]{3,2,1,0:T(8,128)S(1)} %collective-permute-done.4.far_b, ...), custom_call_target="tpu_custom_call" | custom-call | flops 8000000000 | tf_op jit(solution)/shard_map/pallas_call | solution.py:613
  24.1 0.0 copy-start
  24.1 14.7 %all-to-all-start = ((f32[256,1,128]{2,1,0:T(1,128)}), f32[256,1,128]{2,1,0:T(1,128)S(1)}, u32[]{:S(2)}, u32[]{:S(2)}) async-start(f32[256,1,128]{2,1,0:T(1,128)} %bitcast.5), calls=%async_computation | async-start | bytes 262144 | tf_op jit(solution)/shard_map/all_to_all | solution.py:616
  38.8 0.0 collective-permute-done.6.ghost
  38.8 0.0 copy-done
  38.8 1.5 %shard_map.107 = (f32[12,32,128]{2,1,0:T(8,128)S(1)}, f32[12,32,128]{2,1,0:T(8,128)S(1)}, f32[6,16,128]{2,1,0:T(8,128)S(1)}, f32[6,64,128]{2,1,0:T(8,128)S(1)}) custom-call(s32[1]{0:T(128)S(6)} %copy.12.live, s32[128,128]{1,0:T(8,128)S(1)} %bitcast.9, bf16[320,512]{1,0:T(8,128)(2,1)S(1)} %get-tuple-element.37.table, ...), custom_call_target="tpu_custom_call" | custom-call | flops 2000000000 | tf_op jit(solution)/shard_map/pallas_call | solution.py:622
  40.3 1.3 %collective-permute-start.7 = (f32[6,16,128]{2,1,0:T(8,128)S(1)}, f32[6,16,128]{2,1,0:T(8,128)S(1)}, u32[]{:S(2)}, u32[]{:S(2)}) collective-permute-start(f32[6,16,128]{2,1,0:T(8,128)S(1)} %get-tuple-element.42), channel_id=1, source_target_pairs={{8,0},{16,8},{24,16},{32,24},{40,32},{48,40},{56,48},{64,56},{72,6... | collective-permute-start | bytes 147464 | tf_op jit(solution)/shard_map/ppermute | solution.py:636
  41.6 0.7 %shard_map.108.total = f32[6,64,128]{2,1,0:T(8,128)S(1)} custom-call(s32[1]{0:T(128)S(6)} %copy.12.live, s32[128,128]{1,0:T(8,128)S(1)} %bitcast.10, f32[12,32,128]{2,1,0:T(8,128)S(1)} %get-tuple-element.39.parts_p, f32[12,32,128]{2,1,0:T(8,128)S(1)} %get-tuple-element.40.parts_q, f32[6,64,128]{2,1,0:T(8,128)S(1)} %get-tuple-element.41.before), custom_call_target="tpu_custom_call" | custom-call | flops 1000000000 | tf_op jit(solution)/shard_map/pallas_call | solution.py:637
  42.4 4.5 %collective-permute-done.7.returned = f32[6,16,128]{2,1,0:T(8,128)S(1)} collective-permute-done((f32[6,16,128]{2,1,0:T(8,128)S(1)}, f32[6,16,128]{2,1,0:T(8,128)S(1)}, u32[]{:S(2)}, u32[]{:S(2)}) %collective-permute-start.7) | collective-permute-done | bytes 49184 | tf_op jit(solution)/shard_map/ppermute | solution.py:636
  46.8 4.8 %all-to-all-done = f32[256,1,128]{2,1,0:T(1,128)S(1)} async-done(((f32[256,1,128]{2,1,0:T(1,128)}), f32[256,1,128]{2,1,0:T(1,128)S(1)}, u32[]{:S(2)}, u32[]{:S(2)}) %all-to-all-start) | async-done | bytes 131104 | tf_op jit(solution)/shard_map/all_to_all | solution.py:616
  51.6 0.8 %shard_map.109 = (f32[3,8192]{1,0:T(4,128)}, f32[3,8192]{1,0:T(4,128)}, f32[2,8,128]{2,1,0:T(8,128)}) custom-call(f32[6,64,128]{2,1,0:T(8,128)S(1)} %shard_map.108.total, f32[6,16,128]{2,1,0:T(8,128)S(1)} %collective-permute-done.7.returned, f32[3,64,128]{2,1,0:T(8,128)S(1)} %get-tuple-element.43.drag, f32[256,128]{1,0:T(8,128)S(1)} %bitcast.8, ...), custom_call_target="tpu_custom_call" | custom-call | tf_op jit(solution)/shard_map/pallas_call | solution.py:644
  (1 shorter events, 0.0 us)
Async XLA Ops:
  3.4 6.2 %collective-permute-start.1 = (f32[4,2,8,128]{3,2,1,0:T(8,128)S(1)}, f32[4,2,8,128]{3,2,1,0:T(8,128)S(1)}, u32[]{:S(2)}, u32[]{:S(2)}) collective-permute-start(f32[4,2,8,128]{3,2,1,0:T(8,128)S(1)} %get-tuple-element.30.own), channel_id=1, source_target_pairs={{1,2},{2,1},{3,4},{4,3},{5,6},{6,5},{9,10},{10,9},{11,12},{12,11},... | collective-permute-start | bytes 98312 | tf_op jit(solution)/shard_map/ppermute | solution.py:601
  8.0 1.6 %collective-permute-start = (f32[4,2,8,128]{3,2,1,0:T(8,128)S(1)}, f32[4,2,8,128]{3,2,1,0:T(8,128)S(1)}, u32[]{:S(2)}, u32[]{:S(2)}) collective-permute-start(f32[4,2,8,128]{3,2,1,0:T(8,128)S(1)} %get-tuple-element.30.own), channel_id=1, source_target_pairs={{0,1},{1,0},{2,3},{3,2},{4,5},{5,4},{6,7},{7,6},{8,9},{9,8},{10,11... | collective-permute-start | bytes 98312 | tf_op jit(solution)/shard_map/ppermute | solution.py:600
  9.6 13.5 %collective-permute-start.3 = (f32[96,128]{1,0:T(8,128)S(1)}, f32[96,128]{1,0:T(8,128)S(1)}, u32[]{:S(2)}, u32[]{:S(2)}) collective-permute-start(f32[96,128]{1,0:T(8,128)S(1)} %get-tuple-element.34.own), channel_id=1, source_target_pairs={{0,8},{8,0},{16,24},{24,16},{32,40},{40,32},{48,56},{56,48},{64,72... | collective-permute-start | bytes 147464 | tf_op jit(solution)/shard_map/ppermute | solution.py:610
  11.3 11.8 %collective-permute-start.2 = (f32[96,128]{1,0:T(8,128)S(1)}, f32[96,128]{1,0:T(8,128)S(1)}, u32[]{:S(2)}, u32[]{:S(2)}) collective-permute-start(f32[96,128]{1,0:T(8,128)S(1)} %get-tuple-element.34.own), channel_id=1, source_target_pairs={{8,16},{16,8},{24,32},{32,24},{40,48},{48,40},{56,64},{64,56},{72,... | collective-permute-start | bytes 147464 | tf_op jit(solution)/shard_map/ppermute | solution.py:608
  12.0 11.1 %collective-permute-start.5 = (f32[4,2,8,128]{3,2,1,0:T(8,128)S(1)}, f32[4,2,8,128]{3,2,1,0:T(8,128)S(1)}, u32[]{:S(2)}, u32[]{:S(2)}) collective-permute-start(f32[4,2,8,128]{3,2,1,0:T(8,128)S(1)} %get-tuple-element.35), channel_id=1, source_target_pairs={{0,16},{8,24},{16,0},{24,8},{32,48},{40,56},{48,32},{56,40},{64,80... | collective-permute-start | bytes 98312 | tf_op jit(solution)/shard_map/ppermute | solution.py:611
  16.3 6.8 %collective-permute-start.4 = (f32[4,2,8,128]{3,2,1,0:T(8,128)S(1)}, f32[4,2,8,128]{3,2,1,0:T(8,128)S(1)}, u32[]{:S(2)}, u32[]{:S(2)}) collective-permute-start(f32[4,2,8,128]{3,2,1,0:T(8,128)S(1)} %get-tuple-element.35), channel_id=1, source_target_pairs={{16,32},{24,40},{32,16},{40,24},{48,64},{56,72},{64,48},{72,56},{8... | collective-permute-start | bytes 98312 | tf_op jit(solution)/shard_map/ppermute | solution.py:609
  17.6 21.2 %collective-permute-start.6 = (f32[10,16,128]{2,1,0:T(8,128)S(1)}, f32[10,16,128]{2,1,0:T(8,128)S(1)}, u32[]{:S(2)}, u32[]{:S(2)}) collective-permute-start(f32[10,16,128]{2,1,0:T(8,128)S(1)} %get-tuple-element.38), channel_id=1, source_target_pairs={{0,8},{8,16},{16,24},{24,32},{32,40},{40,48},{48,56},{56,64},{64,7... | collective-permute-start | bytes 245768 | tf_op jit(solution)/shard_map/ppermute | solution.py:612
  24.1 14.7 %copy-start = (s32[64,2,128]{2,1,0:T(2,128)S(1)}, s32[64,2,128]{2,1,0:T(2,128)}, u32[]{:S(2)}) copy-start(s32[64,2,128]{2,1,0:T(2,128)} %param.13) | copy-start | bytes 196612
  24.1 27.5 %all-to-all-start = ((f32[256,1,128]{2,1,0:T(1,128)}), f32[256,1,128]{2,1,0:T(1,128)S(1)}, u32[]{:S(2)}, u32[]{:S(2)}) async-start(f32[256,1,128]{2,1,0:T(1,128)} %bitcast.5), calls=%async_computation | async-start | bytes 262144 | tf_op jit(solution)/shard_map/all_to_all | solution.py:616
  40.3 6.5 %collective-permute-start.7 = (f32[6,16,128]{2,1,0:T(8,128)S(1)}, f32[6,16,128]{2,1,0:T(8,128)S(1)}, u32[]{:S(2)}, u32[]{:S(2)}) collective-permute-start(f32[6,16,128]{2,1,0:T(8,128)S(1)} %get-tuple-element.42), channel_id=1, source_target_pairs={{8,0},{16,8},{24,16},{32,24},{40,32},{48,40},{56,48},{64,56},{72,6... | collective-permute-start | bytes 147464 | tf_op jit(solution)/shard_map/ppermute | solution.py:636
